TPU v7x, 128 devices: a whole 4x4x4 slice. The times are simulated.
128 devices in a mesh: batch: 8 (over y, core), frame: 16 (over x, z).
Axes of the slice: x: 4, y: 4, z: 4, core: 2. Of those that a mesh axis runs over, the one named last changes fastest.
Arguments:
- tokens: bfloat16 [8, 32, 256, 1408], P('batch', 'frame'), may hold values from -6 to 6
- frame_time: int32 [8, 32], P('batch'), may hold values from 0 to 31, each once within a row
- valid_count: int32 [8], P('batch'), may hold values from 8 to 32, as said below
- spatial_qkv: bfloat16 [1408, 2112], replicated, may hold values from -0.15625 to 0.15625
- spatial_out: bfloat16 [704, 1408], replicated, may hold values from -0.21875 to 0.21875
- temporal_qkv: bfloat16 [1408, 2112], replicated, may hold values from -0.15625 to 0.15625
- temporal_out: bfloat16 [704, 1408], replicated, may hold values from -0.21875 to 0.21875
- time_embed: float32 [32, 1408], replicated, may hold values from -6 to 6
- video_proj: bfloat16 [1408, 512], replicated, may hold values from -0.15625 to 0.15625
- text_embed: float32 [8, 512], P('batch'), may hold values from -6 to 6
Outputs:
- grad_tokens: bfloat16 [8, 32, 256, 1408], P('batch', 'frame')
- loss: float32 [], replicated
Inputs may be any that keep to these rules, and one draw needn't show every extreme that they name: `frame_time`: each row is a permutation of the time indices 0 to 31. `valid_count`: some clip has all 32 frames valid and another has 8.
All inputs are finite; a program needn't handle non-finite values.
Results may differ from a plain program's by a relative error of at most 0.015.
Values may be sent and summed in bfloat16 or wider, within the bound.
No kernel may reach another device: no remote copies, remote signals or barrier semaphores. Data moves between devices by JAX's collectives and lax.ppermute only.
A program may use at most 128 MiB of HBM per device.

v0:
```python
import functools
import math

import jax
import jax.numpy as jnp
from jax import lax
from jax.experimental import pallas as pl
from jax.experimental.pallas import tpu as pltpu
from jax.sharding import PartitionSpec as P

HEADS = 8
HD = 88
INNER = HEADS * HD
LANES = 128
GROUP = 8
EPSILON = 1e-06
SHARPNESS = 1.0 / 0.07
SCALE = 1.0 / math.sqrt(HD)
MIB = 1024 * 1024

bf16 = jnp.bfloat16
f32 = jnp.float32
VMEM = pl.BlockSpec(memory_space=pltpu.VMEM)
HBM = pl.BlockSpec(memory_space=pltpu.HBM)


def dot_nn(left, right):
    return lax.dot_general(left, right, (((1,), (0,)), ((), ())), preferred_element_type=f32)


def dot_nt(left, right):
    return lax.dot_general(left, right, (((1,), (1,)), ((), ())), preferred_element_type=f32)


def dot_tn(left, right):
    return lax.dot_general(left, right, (((0,), (0,)), ((), ())), preferred_element_type=f32)


def split_terms(values, terms):
    parts = []
    rest = values
    for _ in range(terms):
        part = rest.astype(bf16)
        parts.append(part)
        rest = rest - part.astype(f32)
    return parts


def exact(dot, values, matrix, terms=3):
    rows = values.shape[0]
    products = dot(jnp.concatenate(split_terms(values, terms), axis=0), matrix)
    total = products[:rows]
    for term in range(1, terms):
        total = total + products[term * rows : (term + 1) * rows]
    return total


def window(head):
    first = head * HD // LANES * LANES
    last = min(-(-(head + 1) * HD // LANES) * LANES, INNER)
    return first, last, head * HD - first


def head_lanes(rows, head):
    first, last, offset = window(head)
    lane = lax.broadcasted_iota(jnp.int32, (rows, last - first), 1)
    return (lane >= offset) & (lane < offset + HD)


def keep_head(values, head):
    return jnp.where(head_lanes(values.shape[0], head), values, jnp.zeros_like(values))


def merge_heads(products):
    tiles = []
    for start in range(0, INNER, LANES):
        width = min(LANES, INNER - start)
        tile = None
        for head in range(HEADS):
            first, last, offset = window(head)
            if first <= start < last:
                piece = products[head][:, start - first : start - first + width]
                if tile is None:
                    tile = piece
                else:
                    lane = lax.broadcasted_iota(jnp.int32, piece.shape, 1)
                    tile = jnp.where(lane >= head * HD - start, piece, tile)
        tiles.append(tile)
    return jnp.concatenate(tiles, axis=1)


def normalize(values):
    center = values - jnp.mean(values, axis=-1, keepdims=True)
    spread = jnp.mean(center * center, axis=-1, keepdims=True)
    inverse = lax.rsqrt(spread + EPSILON)
    return center * inverse, inverse


def normalize_back(grad, normed, inverse):
    return inverse * (
        grad
        - jnp.mean(grad, axis=-1, keepdims=True)
        - normed * jnp.mean(grad * normed, axis=-1, keepdims=True)
    )


def spatial_norm(count_ref, tok_ref, xn_ref, inverse_ref, count_out_ref):
    count_out_ref[...] = count_ref[...]
    for frame in range(tok_ref.shape[0]):
        normed, inverse = normalize(tok_ref[frame].astype(f32))
        xn_ref[frame] = normed.astype(bf16)
        inverse_ref[frame] = inverse


def spatial_forward(tok_ref, xn_ref, qkv_ref, out_ref, x1_ref, q_ref, k_ref, v_ref, p_ref):
    frames, patches, _ = tok_ref.shape
    owners = x1_ref.shape[0]
    share = patches // owners
    for frame in range(frames):
        for i, held_ref in enumerate((q_ref, k_ref, v_ref)):
            part = qkv_ref[i * INNER : (i + 1) * INNER, :]
            held_ref[frame] = dot_nt(xn_ref[frame], part).astype(bf16)
        mixed = []
        for head in range(HEADS):
            first, last, _ = window(head)
            query = keep_head(q_ref[frame, :, first:last], head)
            raised = jnp.exp(dot_nt(query, k_ref[frame, :, first:last]) * SCALE)
            weights = (raised * (1.0 / jnp.sum(raised, axis=-1, keepdims=True))).astype(bf16)
            p_ref[frame, head] = weights
            mixed.append(dot_nn(weights, v_ref[frame, :, first:last]))
        update = dot_nn(merge_heads(mixed).astype(bf16), out_ref[...])
        x1 = (tok_ref[frame].astype(f32) + update).astype(bf16)
        own = slice(frame * share, (frame + 1) * share)
        x1_ref[:, own, :] = x1.reshape(owners, share, x1.shape[-1])


def spatial_backward(
    grad_ref,
    xn_ref,
    inverse_ref,
    qkv_ref,
    out_ref,
    q_ref,
    k_ref,
    v_ref,
    p_ref,
    result_hbm,
    result_ref,
    result_sem,
):
    frames, patches, width = xn_ref.shape
    owners = grad_ref.shape[0]
    share = patches // owners
    copies = []
    for frame in range(frames):
        own = slice(frame * share, (frame + 1) * share)
        grad_x1 = grad_ref[:, own, :].reshape(patches, width)
        grad_so = dot_nt(grad_x1, out_ref[...]).astype(bf16)
        dq, dk, dv = [], [], []
        for head in range(HEADS):
            first, last, _ = window(head)
            grad_head = grad_so[:, first:last]
            weights = p_ref[frame, head]
            grad_weights = dot_nt(keep_head(grad_head, head), v_ref[frame, :, first:last])
            wide = weights.astype(f32)
            inner = jnp.sum(grad_weights * wide, axis=-1, keepdims=True)
            grad_scores = (wide * (grad_weights - inner) * SCALE).astype(bf16)
            dq.append(dot_nn(grad_scores, k_ref[frame, :, first:last]))
            dk.append(dot_tn(grad_scores, q_ref[frame, :, first:last]))
            dv.append(dot_tn(weights, grad_head))
        grad_xn = dot_nn(merge_heads(dq).astype(bf16), qkv_ref[:INNER, :])
        grad_xn += dot_nn(merge_heads(dk).astype(bf16), qkv_ref[INNER : 2 * INNER, :])
        grad_xn += dot_nn(merge_heads(dv).astype(bf16), qkv_ref[2 * INNER :, :])
        back = normalize_back(grad_xn, xn_ref[frame].astype(f32), inverse_ref[frame])
        grad_x1 = grad_ref[:, own, :].reshape(patches, width)
        result_ref[frame] = (grad_x1.astype(f32) + back).astype(bf16)
        copy = pltpu.make_async_copy(
            result_ref.at[frame], result_hbm.at[frame], result_sem.at[frame]
        )
        copy.start()
        copies.append(copy)
    for copy in copies:
        copy.wait()


def slot_columns(times_row, count, rows):
    slots = times_row.shape[1]
    valid = jnp.where(times_row < count, 1.0, 0.0).astype(f32)
    row_slot = lax.broadcasted_iota(jnp.int32, (rows, slots), 0) // GROUP
    slot = lax.broadcasted_iota(jnp.int32, (rows, slots), 1)
    column = jnp.sum(jnp.where(row_slot == slot, valid, 0.0), axis=1, keepdims=True)
    return valid, column


def temporal_forward(
    count_ref,
    row_ref,
    x1_ref,
    embed_ref,
    qkv_ref,
    out_ref,
    proj_ref,
    text_ref,
    send_ref,
    tn_ref,
    inverse_ref,
    q_ref,
    k_ref,
    p_ref,
    c_ref,
):
    slots, share, width = x1_ref.shape
    groups = share // GROUP
    rows = slots * GROUP
    count = count_ref[...]
    lookup = jnp.where(
        lax.broadcasted_iota(jnp.int32, (embed_ref.shape[0], slots), 0) == row_ref[...], 1.0, 0.0
    ).astype(bf16)
    added = None
    for part in split_terms(embed_ref[...], 3):
        term = dot_tn(lookup, part)
        added = term if added is None else added + term
    valid, valid_column = slot_columns(row_ref[...], count, rows)
    chunk = 8
    pooled = jnp.zeros((1, width), f32)
    for start in range(0, slots, chunk):
        y = x1_ref[start : start + chunk].astype(f32) + added[start : start + chunk][:, None, :]
        part = jnp.sum(y, axis=1)
        slot_valid = jnp.concatenate(
            [valid_column[(start + i) * GROUP : (start + i) * GROUP + 1] for i in range(chunk)],
            axis=0,
        )
        pooled = pooled + jnp.sum(part * slot_valid, axis=0, keepdims=True)
        normed, inverse = normalize(y)
        for group in range(groups):
            own = slice(group * GROUP, (group + 1) * GROUP)
            at = pl.ds(group * rows + start * GROUP, chunk * GROUP)
            tn_ref[at, :] = normed[:, own, :].reshape(chunk * GROUP, width).astype(bf16)
            inverse_ref[at, :] = inverse[:, own, :].reshape(chunk * GROUP, 1)
    row_index = lax.broadcasted_iota(jnp.int32, (rows, rows), 0)
    column_index = lax.broadcasted_iota(jnp.int32, (rows, rows), 1)
    spread = jnp.where(
        lax.broadcasted_iota(jnp.int32, (slots, rows), 0)
        == lax.broadcasted_iota(jnp.int32, (slots, rows), 1) // GROUP,
        1.0,
        0.0,
    ).astype(bf16)
    key_valid = dot_nn(jnp.broadcast_to(valid, (GROUP, slots)).astype(bf16), spread)[:1]
    allowed = (row_index % GROUP == column_index % GROUP) & (key_valid > 0.5)
    for group in range(groups):
        at = pl.ds(group * rows, rows)
        q_ref[at, :] = dot_nt(tn_ref[at, :], qkv_ref[:INNER, :]).astype(bf16)
        k_ref[at, :] = dot_nt(tn_ref[at, :], qkv_ref[INNER : 2 * INNER, :]).astype(bf16)
        for head in range(HEADS):
            first, last, _ = window(head)
            query = keep_head(q_ref[at, first:last], head)
            scores = dot_nt(query, k_ref[at, first:last]) * SCALE
            raised = jnp.where(allowed, jnp.exp(scores), 0.0)
            weights = raised * (valid_column / jnp.sum(raised, axis=-1, keepdims=True))
            p_ref[group, head] = weights.astype(bf16)
            c_ref[head : head + 1, at] = jnp.sum(weights, axis=0, keepdims=True)
    gathered = exact(dot_nn, c_ref[...], tn_ref[...], 2)
    mixed_all = exact(dot_nt, gathered, qkv_ref[2 * INNER :, :])
    lane = lax.broadcasted_iota(jnp.int32, mixed_all.shape, 1)
    head_row = lax.broadcasted_iota(jnp.int32, mixed_all.shape, 0)
    own_lane = (lane >= head_row * HD) & (lane < head_row * HD + HD)
    mixed = jnp.sum(jnp.where(own_lane, mixed_all, 0.0), axis=0, keepdims=True)
    feature = pooled + exact(dot_nn, jnp.broadcast_to(mixed, (GROUP, INNER)), out_ref[...])[:1]
    z = exact(dot_nn, jnp.broadcast_to(feature, (GROUP, width)), proj_ref[...])[:1]
    z = z / (count.astype(f32) * float(PATCHES))
    embed_size = z.shape[1]
    send_ref[:, :, :embed_size] = jnp.broadcast_to(
        z[None], (send_ref.shape[0], 1, embed_size)
    )
    tiles = embed_size // LANES
    own_tile = lax.axis_index("frame") // (lax.axis_size("frame") // tiles)
    piece = jnp.zeros((1, LANES), f32)
    for tile in range(tiles):
        held = text_ref[:, tile * LANES : (tile + 1) * LANES]
        piece = jnp.where(own_tile == tile, held, piece)
    send_ref[:, :, embed_size:] = jnp.broadcast_to(piece[None], (send_ref.shape[0], 1, LANES))


PATCHES = 256


def unit_rows(matrix):
    inverse = lax.rsqrt(jnp.sum(matrix * matrix, axis=-1, keepdims=True) + EPSILON)
    return matrix * inverse, inverse


def temporal_backward(
    batch,
    cotangent,
    count_ref,
    row_ref,
    parts_ref,
    tn_ref,
    inverse_ref,
    q_ref,
    k_ref,
    p_ref,
    c_ref,
    qkv_ref,
    out_ref,
    proj_ref,
    grad_ref,
    loss_ref,
    dtn_ref,
):
    slots, share, width = grad_ref.shape
    groups = share // GROUP
    rows = slots * GROUP
    count = count_ref[...]
    clips = batch
    per_clip = parts_ref.shape[0] // clips
    embed_size = proj_ref.shape[1]
    parts = parts_ref[:, 0, :].reshape(clips, per_clip, parts_ref.shape[2])
    z = jnp.sum(parts[:, :, :embed_size], axis=1)
    tiles = embed_size // LANES
    text = jnp.concatenate(
        [parts[:, i * (per_clip // tiles), embed_size:] for i in range(tiles)], axis=1
    )
    e, inverse_z = unit_rows(z)
    u, _ = unit_rows(text)
    logits = (
        lax.dot_general(
            e,
            u,
            (((1,), (1,)), ((), ())),
            precision=lax.Precision.HIGHEST,
            preferred_element_type=f32,
        )
        * SHARPNESS
    )
    raised = jnp.exp(logits)
    row_total = jnp.sum(raised, axis=1, keepdims=True)
    column_total = jnp.sum(raised, axis=0, keepdims=True)
    diagonal = lax.broadcasted_iota(jnp.int32, logits.shape, 0) == lax.broadcasted_iota(
        jnp.int32, logits.shape, 1
    )
    loss = (
        0.5 * jnp.sum(jnp.log(row_total), axis=0, keepdims=True)
        + 0.5 * jnp.sum(jnp.log(column_total), axis=1, keepdims=True)
        - jnp.sum(jnp.sum(jnp.where(diagonal, logits, 0.0), axis=1, keepdims=True), axis=0, keepdims=True)
    )
    loss_ref[...] = loss
    shares = 0.5 * (raised / row_total + raised / column_total) - jnp.where(diagonal, 1.0, 0.0)
    grad_e = (cotangent * SHARPNESS) * lax.dot_general(
        shares,
        u,
        (((1,), (0,)), ((), ())),
        precision=lax.Precision.HIGHEST,
        preferred_element_type=f32,
    )
    grad_z = inverse_z * (grad_e - e * jnp.sum(e * grad_e, axis=-1, keepdims=True))
    own = lax.broadcasted_iota(jnp.int32, grad_z.shape, 0) == lax.axis_index("batch")
    grad_own = jnp.sum(jnp.where(own, grad_z, 0.0), axis=0, keepdims=True)
    grad_own = grad_own / (count.astype(f32) * float(PATCHES))
    grad_feature = exact(dot_nt, jnp.broadcast_to(grad_own, grad_z.shape), proj_ref[...])
    grad_mixed = exact(dot_nt, grad_feature, out_ref[...])
    lane = lax.broadcasted_iota(jnp.int32, grad_mixed.shape, 1)
    head_row = lax.broadcasted_iota(jnp.int32, grad_mixed.shape, 0)
    own_lane = (lane >= head_row * HD) & (lane < head_row * HD + HD)
    value_grad = exact(dot_nn, jnp.where(own_lane, grad_mixed, 0.0), qkv_ref[2 * INNER :, :])
    high, low = split_terms(value_grad, 2)
    scores_grad = exact(dot_nt, value_grad, tn_ref[...], 2)
    c_high, c_low = split_terms(c_ref[...], 2)
    _, valid_column = slot_columns(row_ref[...], count, rows)
    for group in range(groups):
        at = pl.ds(group * rows, rows)
        dq, dk = [], []
        for head in range(HEADS):
            first, last, _ = window(head)
            weights = p_ref[group, head].astype(f32)
            along = scores_grad[head : head + 1, group * rows : (group + 1) * rows]
            inner = jnp.sum(weights * along, axis=-1, keepdims=True)
            grad_scores = (weights * (along - inner) * SCALE).astype(bf16)
            dq.append(dot_nn(grad_scores, k_ref[at, first:last]))
            dk.append(dot_tn(grad_scores, q_ref[at, first:last]))
        own = slice(group * rows, (group + 1) * rows)
        weights_c = jnp.concatenate([c_high[:, own], c_high[:, own], c_low[:, own]], axis=0)
        value_rows = jnp.concatenate([high, low, high], axis=0)
        grad_tn = dot_nn(merge_heads(dq).astype(bf16), qkv_ref[:INNER, :])
        grad_tn += dot_nn(merge_heads(dk).astype(bf16), qkv_ref[INNER : 2 * INNER, :])
        dtn_ref[at, :] = grad_tn + dot_tn(weights_c, value_rows)
    chunk = 8
    for start in range(0, slots, chunk):
        pieces = []
        for group in range(groups):
            at = pl.ds(group * rows + start * GROUP, chunk * GROUP)
            back = normalize_back(dtn_ref[at, :], tn_ref[at, :].astype(f32), inverse_ref[at, :])
            back = (
                back
                + valid_column[start * GROUP : (start + chunk) * GROUP] * grad_feature[:1]
            )
            pieces.append(back.reshape(chunk, 1, GROUP, width))
        joined = jnp.concatenate(pieces, axis=1).reshape(chunk, share, width)
        grad_ref[start : start + chunk] = joined.astype(bf16)


def cost(microseconds):
    return pl.CostEstimate(flops=microseconds * 10**9, bytes_accessed=0, transcendentals=0)


def per_device(
    tokens,
    frame_time,
    valid_count,
    spatial_qkv,
    spatial_out,
    temporal_qkv,
    temporal_out,
    time_embed,
    video_proj,
    text_embed,
):
    frames_in = tokens[0]
    local_frames, patches, width = frames_in.shape
    owners = lax.axis_size("frame")
    clips = lax.axis_size("batch")
    devices = owners * clips
    share = patches // owners
    slots = owners * local_frames
    groups = share // GROUP
    rows = slots * share
    shape = jax.ShapeDtypeStruct
    traded = (owners, local_frames * share, width)
    params = pltpu.CompilerParams(vmem_limit_bytes=20 * MIB)
    spatial_qkv = spatial_qkv.T
    temporal_qkv = temporal_qkv.T
    counts = valid_count.reshape(1, 1)

    xn, xn_inverse, counts = pl.pallas_call(
        spatial_norm,
        out_shape=(
            shape(frames_in.shape, bf16),
            shape((local_frames, patches, 1), f32),
            shape((1, 1), jnp.int32),
        ),
        in_specs=[VMEM] * 2,
        out_specs=(VMEM,) * 3,
        compiler_params=params,
        cost_estimate=cost(1),
        name="spatial_norm",
    )(counts, frames_in)
    x1, q, k, v, p = pl.pallas_call(
        spatial_forward,
        out_shape=(
            shape(traded, bf16),
            shape((local_frames, patches, INNER), bf16),
            shape((local_frames, patches, INNER), bf16),
            shape((local_frames, patches, INNER), bf16),
            shape((local_frames, HEADS, patches, patches), bf16),
        ),
        in_specs=[VMEM] * 4,
        out_specs=(VMEM,) * 5,
        compiler_params=params,
        cost_estimate=cost(8),
        name="spatial_forward",
    )(frames_in, xn, spatial_qkv, spatial_out)

    x1 = lax.all_to_all(x1, "frame", split_axis=0, concat_axis=0, tiled=True)
    x1 = x1.reshape(slots, share, width)
    embed_size = text_embed.shape[1]
    send, tn, inverse, tq, tk, tp, c = pl.pallas_call(
        temporal_forward,
        out_shape=(
            shape((devices, 1, embed_size + LANES), f32),
            shape((rows, width), bf16),
            shape((rows, 1), f32),
            shape((rows, INNER), bf16),
            shape((rows, INNER), bf16),
            shape((groups, HEADS, slots * GROUP, slots * GROUP), bf16),
            shape((HEADS, rows), f32),
        ),
        in_specs=[VMEM] * 8,
        out_specs=(VMEM,) * 7,
        compiler_params=params,
        cost_estimate=cost(7),
        name="temporal_forward",
    )(
        counts,
        frame_time,
        x1,
        time_embed,
        temporal_qkv,
        temporal_out,
        video_proj,
        text_embed,
    )

    parts = lax.all_to_all(send, ("batch", "frame"), split_axis=0, concat_axis=0, tiled=True)
    grad_x1, loss = pl.pallas_call(
        functools.partial(temporal_backward, clips, float(slots * patches)),
        out_shape=(shape((slots, share, width), bf16), shape((1, 1), f32)),
        in_specs=[VMEM] * 12,
        out_specs=(VMEM,) * 2,
        scratch_shapes=[pltpu.VMEM((rows, width), f32)],
        compiler_params=params,
        cost_estimate=cost(8),
        name="temporal_backward",
    )(
        counts,
        frame_time,
        parts,
        tn,
        inverse,
        tq,
        tk,
        tp,
        c,
        temporal_qkv,
        temporal_out,
        video_proj,
    )
    grad_x1 = lax.all_to_all(
        grad_x1.reshape(traded), "frame", split_axis=0, concat_axis=0, tiled=True
    )
    result = pl.pallas_call(
        spatial_backward,
        out_shape=shape(frames_in.shape, bf16),
        in_specs=[VMEM] * 9,
        out_specs=HBM,
        scratch_shapes=[
            pltpu.VMEM(frames_in.shape, bf16),
            pltpu.SemaphoreType.DMA((local_frames,)),
        ],
        compiler_params=params,
        cost_estimate=cost(12),
        name="spatial_backward",
    )(grad_x1, xn, xn_inverse, spatial_qkv, spatial_out, q, k, v, p)
    return (result[None], loss[0, 0])


def solution(mesh):
    placed = (
        P("batch", "frame", None, None),
        P("batch", None),
        P("batch"),
        P(),
        P(),
        P(),
        P(),
        P(),
        P(),
        P("batch", None),
    )
    return jax.shard_map(
        per_device,
        mesh=mesh,
        in_specs=placed,
        out_specs=(P("batch", "frame", None, None), P()),
        check_vma=False,
    )
```

profile of v0, /device:TPU:0, one launch (start us, length us, event | category | flops | bytes accessed | tf_op | source)
XLA Modules:
  0.0 116.6 jit_solution(15539482335183996409)
XLA Ops:
  1.3 0.0 copy-start.4
  1.3 1.4 %copy-done.4 = bf16[1,2,256,1408]{3,2,1,0:T(8,128)(2,1)S(1)} copy-done((bf16[1,2,256,1408]{3,2,1,0:T(8,128)(2,1)S(1)}, bf16[1,2,256,1408]{3,2,1,0:T(8,128)(2,1)}, u32[]{:S(2)}) %copy-start.4) | copy-done | bytes 1441816
  2.6 0.0 slice-start
  2.6 1.3 %spatial_norm.1 = (bf16[2,256,1408]{2,1,0:T(8,128)(2,1)S(1)}, f32[2,256,1]{2,1,0:T(8,128)S(1)}, s32[1,1]{1,0:T(1,128)}) custom-call(s32[1,1]{1,0:T(1,128)} %bitcast.8.count_ref, bf16[2,256,1408]{2,1,0:T(8,128)(2,1)S(1)} %bitcast.19), custom_call_target="tpu_custom_call" | custom-call | flops 1000000000 | tf_op jit(solution)/shard_map/spatial_norm/pallas_call | solution.py:434
  3.9 2.7 %copy-done = bf16[1408,2112]{0,1:T(8,128)(2,1)S(1)} copy-done((bf16[1408,2112]{0,1:T(8,128)(2,1)S(1)}, bf16[1408,2112]{0,1:T(8,128)(2,1)}, u32[]{:S(2)}) %copy-start) | copy-done | bytes 5947416
  6.6 0.0 copy-start.2
  6.6 1.5 %copy-done.2 = bf16[704,1408]{1,0:T(8,128)(2,1)S(1)} copy-done((bf16[704,1408]{1,0:T(8,128)(2,1)S(1)}, bf16[704,1408]{1,0:T(8,128)(2,1)}, u32[]{:S(2)}) %copy-start.2) | copy-done | bytes 1982488
  8.2 0.0 slice-start.1
  8.2 0.0 copy-start.5
  8.2 7.3 %spatial_forward.1 = (bf16[16,32,1408]{2,1,0:T(8,128)(2,1)S(1)}, bf16[2,256,704]{2,1,0:T(8,128)(2,1)S(1)}, bf16[2,256,704]{2,1,0:T(8,128)(2,1)S(1)}, bf16[2,256,...) custom-call(bf16[2,256,1408]{2,1,0:T(8,128)(2,1)S(1)} %bitcast.20, bf16[2,256,1408]{2,1,0:T(8,128)(2,1)S(1)} %get-tuple-element.20.xn_ref, ...), custom_call_target="tpu_custom_call" | custom-call | flops 8000000000 | tf_op jit(solution)/shard_map/spatial_forward/pallas_call | solution.py:447
  15.5 0.0 copy-start.1
  15.5 0.0 copy-start.6
  15.5 0.0 copy-start.7
  15.5 0.0 copy-start.8
  15.5 28.9 %all_to_all.15 = bf16[16,32,1408]{2,1,0:T(8,128)(2,1)S(1)} all-to-all(bf16[16,32,1408]{2,1,0:T(8,128)(2,1)S(1)} %get-tuple-element.21), channel_id=1, replica_groups=mesh['batch'=8,'frame'=16] {'frame'}, dimensions={0} | all-to-all | bytes 2883584 | tf_op jit(solution)/shard_map/all_to_all | solution.py:463
  44.5 0.0 slice-done
  44.5 0.0 slice-done.1
  44.5 0.0 copy-done.5
  44.5 0.0 copy-done.1
  44.5 0.0 copy-done.6
  44.5 0.0 copy-done.7
  44.5 0.0 copy-done.8
  44.5 0.0 slice-start.2
  44.5 7.7 %temporal_forward.1 = (f32[128,1,640]{2,1,0:T(1,128)S(1)}, bf16[512,1408]{1,0:T(8,128)(2,1)S(1)}, f32[512,1]{1,0:T(8,128)S(1)}, bf16[512,704]{1,0:T(8,128)(2,1)S...) custom-call(s32[1,1]{1,0:T(1,128)} %get-tuple-element.19.count_ref, ...), custom_call_target="tpu_custom_call" | custom-call | flops 7000000000 | tf_op jit(solution)/shard_map/temporal_forward/pallas_call | solution.py:466
  52.3 18.4 %all_to_all.16.parts_ref = f32[128,1,640]{2,1,0:T(1,128)S(1)} all-to-all(f32[128,1,640]{2,1,0:T(1,128)S(1)} %get-tuple-element.22), channel_id=1, replica_groups=mesh['batch'=8,'frame'=16] {'batch','frame'}, dimensions={0} | all-to-all | bytes 655360 | tf_op jit(solution)/shard_map/all_to_all | solution.py:493
  70.7 9.0 %temporal_backward.1 = (bf16[32,16,1408]{2,1,0:T(8,128)(2,1)S(1)}, f32[1,1]{1,0:T(1,128)}) custom-call(s32[1,1]{1,0:T(1,128)} %get-tuple-element.19.count_ref, s32[1,32]{1,0:T(1,128)S(1)} %copy-done.8, f32[128,1,640]{2,1,0:T(1,128)S(1)} %all_to_all.16.parts_ref, bf16[512,1408]{1,0:T(8,128)(2,1)S(1)} %get-tuple-element.23.tn_ref, ...), custom_call_target="tpu_custom_call" | custom-call | flops 8000000000 | tf_op jit(solution)/shard_map/temporal_backward/pallas_call | solution.py:494
  79.7 0.0 copy-start.3
  79.7 23.8 %all_to_all.17.grad_ref = bf16[16,32,1408]{2,1,0:T(8,128)(2,1)S(1)} all-to-all(bf16[16,32,1408]{2,1,0:T(8,128)(2,1)S(1)} %bitcast.9), channel_id=1, replica_groups=mesh['batch'=8,'frame'=16] {'frame'}, dimensions={0} | all-to-all | bytes 2883584 | tf_op jit(solution)/shard_map/all_to_all | solution.py:517
  103.5 0.0 slice-done.2
  103.5 0.0 slice-done.3
  103.5 0.0 copy-done.3
  103.5 12.9 %spatial_backward.1 = bf16[2,256,1408]{2,1,0:T(8,128)(2,1)} custom-call(bf16[16,32,1408]{2,1,0:T(8,128)(2,1)S(1)} %all_to_all.17.grad_ref, bf16[2,256,1408]{2,1,0:T(8,128)(2,1)S(1)} %get-tuple-element.20.xn_ref, f32[2,256,1]{2,1,0:T(8,128)S(1)} %get-tuple-element.30.inverse_ref, bf16[2112,1408]{1,0:T(8,128)(2,1)S(1)} %bitcast.18, ...), custom_call_target="tpu_custom_call" | custom-call | flops 12000000000 | tf_op jit(solution)/shard_map/spatial_backward/pallas_call | solution.py:520
  (4 shorter events, 0.0 us)
Async XLA Ops:
  1.3 1.4 %copy-start.4 = (bf16[1,2,256,1408]{3,2,1,0:T(8,128)(2,1)S(1)}, bf16[1,2,256,1408]{3,2,1,0:T(8,128)(2,1)}, u32[]{:S(2)}) copy-start(bf16[1,2,256,1408]{3,2,1,0:T(8,128)(2,1)} %param.10) | copy-start | bytes 4325380
  2.6 41.8 %slice-start = ((s8[5947392]{0:T(1024)(128)(4,1)}), s8[4194304]{0:T(1024)(128)(4,1)S(1)}, s32[]{:S(2)}) async-start(s8[5947392]{0:T(1024)(128)(4,1)} %bitcast.11), calls=%async_computation.3 | async-start | bytes 8388608
  3.9 2.7 %copy-start = (bf16[1408,2112]{0,1:T(8,128)(2,1)S(1)}, bf16[1408,2112]{0,1:T(8,128)(2,1)}, u32[]{:S(2)}) copy-start(bf16[1408,2112]{0,1:T(8,128)(2,1)} %param.13) | copy-start | bytes 17842180
  6.6 1.6 %copy-start.2 = (bf16[704,1408]{1,0:T(8,128)(2,1)S(1)}, bf16[704,1408]{1,0:T(8,128)(2,1)}, u32[]{:S(2)}) copy-start(bf16[704,1408]{1,0:T(8,128)(2,1)} %out_ref.7) | copy-start | bytes 5947396
  8.2 36.3 %slice-start.1 = ((s8[5947392]{0:T(1024)(128)(4,1)}), s8[1753088]{0:T(1024)(128)(4,1)S(1)}, s32[]{:S(2)}) async-start(s8[5947392]{0:T(1024)(128)(4,1)} %bitcast.11), calls=%async_computation.4 | async-start | bytes 3506176
  8.2 36.3 %copy-start.5 = (bf16[1408,512]{1,0:T(8,128)(2,1)S(1)}, bf16[1408,512]{1,0:T(8,128)(2,1)}, u32[]{:S(2)}) copy-start(bf16[1408,512]{1,0:T(8,128)(2,1)} %proj_ref.3) | copy-start | bytes 4325380
  15.5 29.0 %copy-start.1 = (bf16[704,1408]{1,0:T(8,128)(2,1)S(1)}, bf16[704,1408]{1,0:T(8,128)(2,1)}, u32[]{:S(2)}) copy-start(bf16[704,1408]{1,0:T(8,128)(2,1)} %out_ref.6) | copy-start | bytes 5947396
  15.5 29.0 %copy-start.6 = (f32[32,1408]{1,0:T(8,128)S(1)}, f32[32,1408]{1,0:T(8,128)}, u32[]{:S(2)}) copy-start(f32[32,1408]{1,0:T(8,128)} %embed_ref.1) | copy-start | bytes 540676
  15.5 29.0 %copy-start.7 = (f32[1,512]{1,0:T(1,128)S(1)}, f32[1,512]{1,0:T(1,128)}, u32[]{:S(2)}) copy-start(f32[1,512]{1,0:T(1,128)} %text_ref.1) | copy-start | bytes 6148
  15.5 29.0 %copy-start.8 = (s32[1,32]{1,0:T(1,128)S(1)}, s32[1,32]{1,0:T(1,128)}, u32[]{:S(2)}) copy-start(s32[1,32]{1,0:T(1,128)} %row_ref.3) | copy-start | bytes 388
  44.5 58.9 %slice-start.2 = ((s8[5947392]{0:T(1024)(128)(4,1)}), s8[4194304]{0:T(1024)(128)(4,1)S(1)}, s32[]{:S(2)}) async-start(s8[5947392]{0:T(1024)(128)(4,1)} %bitcast.16), calls=%async_computation.5 | async-start | bytes 8388608
  70.7 32.8 %slice-start.3 = ((s8[5947392]{0:T(1024)(128)(4,1)}), s8[1753088]{0:T(1024)(128)(4,1)S(1)}, s32[]{:S(2)}) async-start(s8[5947392]{0:T(1024)(128)(4,1)} %bitcast.16), calls=%async_computation.6 | async-start | bytes 3506176
  79.7 23.8 %copy-start.3 = (bf16[704,1408]{1,0:T(8,128)(2,1)S(1)}, bf16[704,1408]{1,0:T(8,128)(2,1)}, u32[]{:S(2)}) copy-start(bf16[704,1408]{1,0:T(8,128)(2,1)} %out_ref.7) | copy-start | bytes 5947396
where the time goes:
time: 117 us
  blocking collectives  71.1 us (61%)
  Pallas kernels  38.2 us (33%)
  local copies, waits for them, and re-layouts  5.65 us (5%)
  between operations  1.62 us (1%)
    all_to_all x1, blocking collectives, per_device(): x1 = lax.all_to_all(x1, 'frame', split_axis=0, concat_axis=0, tiled=True)  28.9 us
    all_to_all x1, blocking collectives, per_device(): lax.all_to_all(grad_x1.reshape(traded), 'frame', split_axis=0, concat_axi...  23.8 us
    all_to_all x1, blocking collectives, per_device(): lax.all_to_all(send, ('batch', 'frame'), split_axis=0, concat_axis=0, til...  18.4 us
    pallas_call x1, Pallas kernels, per_device(): pl.pallas_call(spatial_backward, out_shape=shape(frames_in.shape, bf16),...  12.9 us
    pallas_call x1, Pallas kernels, per_device(): pl.pallas_call(functools.partial(temporal_backward, clips, float(slots *...  9 us
    pallas_call x1, Pallas kernels, per_device(): pl.pallas_call(temporal_forward, out_shape=(shape((devices, 1, embed_size...  7.73 us
    pallas_call x1, Pallas kernels, per_device(): pl.pallas_call(spatial_forward, out_shape=(shape(traded, bf16), shape((lo...  7.27 us
    unnamed x26, local copies, waits for them, and re-layouts  5.65 us

commit v1 on v0

--- a/solution.py
+++ b/solution.py
@@ -16,6 +16,8 @@
 EPSILON = 1e-06
 SHARPNESS = 1.0 / 0.07
 SCALE = 1.0 / math.sqrt(HD)
+QUERY_SCALE = SCALE / math.log(2.0)
+KEY_BACK = math.log(2.0)
 MIB = 1024 * 1024
 
 bf16 = jnp.bfloat16
@@ -112,23 +114,32 @@
         inverse_ref[frame] = inverse
 
 
-def spatial_forward(tok_ref, xn_ref, qkv_ref, out_ref, x1_ref, q_ref, k_ref, v_ref, p_ref):
+def spatial_forward(
+    tok_ref, xn_ref, qkv_ref, out_ref, x1_ref, q_ref, k_ref, v_ref, p_ref, so_ref
+):
     frames, patches, _ = tok_ref.shape
     owners = x1_ref.shape[0]
     share = patches // owners
     for frame in range(frames):
-        for i, held_ref in enumerate((q_ref, k_ref, v_ref)):
-            part = qkv_ref[i * INNER : (i + 1) * INNER, :]
-            held_ref[frame] = dot_nt(xn_ref[frame], part).astype(bf16)
+        packed = dot_nt(xn_ref[frame], qkv_ref[...])
+        q_ref[frame] = (packed[:, :INNER] * QUERY_SCALE).astype(bf16)
+        k_ref[frame] = packed[:, INNER : 2 * INNER].astype(bf16)
+        v_ref[frame] = packed[:, 2 * INNER :].astype(bf16)
+        scores = []
+        for head in range(HEADS):
+            first, last, _ = window(head)
+            query = keep_head(q_ref[frame, :, first:last], head)
+            scores.append(dot_nt(query, k_ref[frame, :, first:last]))
+        for head in range(HEADS):
+            raised = jnp.exp2(scores[head])
+            weights = raised * (1.0 / jnp.sum(raised, axis=-1, keepdims=True))
+            p_ref[frame, head] = weights.astype(bf16)
         mixed = []
         for head in range(HEADS):
             first, last, _ = window(head)
-            query = keep_head(q_ref[frame, :, first:last], head)
-            raised = jnp.exp(dot_nt(query, k_ref[frame, :, first:last]) * SCALE)
-            weights = (raised * (1.0 / jnp.sum(raised, axis=-1, keepdims=True))).astype(bf16)
-            p_ref[frame, head] = weights
-            mixed.append(dot_nn(weights, v_ref[frame, :, first:last]))
-        update = dot_nn(merge_heads(mixed).astype(bf16), out_ref[...])
+            mixed.append(dot_nn(p_ref[frame, head], v_ref[frame, :, first:last]))
+        so_ref[frame] = merge_heads(mixed).astype(bf16)
+        update = dot_nn(so_ref[frame], out_ref[...])
         x1 = (tok_ref[frame].astype(f32) + update).astype(bf16)
         own = slice(frame * share, (frame + 1) * share)
         x1_ref[:, own, :] = x1.reshape(owners, share, x1.shape[-1])
@@ -144,6 +155,7 @@
     k_ref,
     v_ref,
     p_ref,
+    so_ref,
     result_hbm,
     result_ref,
     result_sem,
@@ -156,21 +168,28 @@
         own = slice(frame * share, (frame + 1) * share)
         grad_x1 = grad_ref[:, own, :].reshape(patches, width)
         grad_so = dot_nt(grad_x1, out_ref[...]).astype(bf16)
-        dq, dk, dv = [], [], []
-        for head in range(HEADS):
-            first, last, _ = window(head)
-            grad_head = grad_so[:, first:last]
-            weights = p_ref[frame, head]
-            grad_weights = dot_nt(keep_head(grad_head, head), v_ref[frame, :, first:last])
-            wide = weights.astype(f32)
-            inner = jnp.sum(grad_weights * wide, axis=-1, keepdims=True)
-            grad_scores = (wide * (grad_weights - inner) * SCALE).astype(bf16)
+        dv = []
+        for head in range(HEADS):
+            first, last, _ = window(head)
+            dv.append(dot_tn(p_ref[frame, head], grad_so[:, first:last]))
+        dv = merge_heads(dv).astype(bf16)
+        grad_weights, inner = [], []
+        for head in range(HEADS):
+            first, last, _ = window(head)
+            grad_head = keep_head(grad_so[:, first:last], head)
+            along = grad_head.astype(f32) * so_ref[frame, :, first:last].astype(f32)
+            inner.append(jnp.sum(along, axis=-1, keepdims=True))
+            grad_weights.append(dot_nt(grad_head, v_ref[frame, :, first:last]))
+        dq, dk = [], []
+        for head in range(HEADS):
+            first, last, _ = window(head)
+            weights = p_ref[frame, head].astype(f32)
+            grad_scores = (weights * (grad_weights[head] - inner[head])).astype(bf16)
             dq.append(dot_nn(grad_scores, k_ref[frame, :, first:last]))
             dk.append(dot_tn(grad_scores, q_ref[frame, :, first:last]))
-            dv.append(dot_tn(weights, grad_head))
-        grad_xn = dot_nn(merge_heads(dq).astype(bf16), qkv_ref[:INNER, :])
-        grad_xn += dot_nn(merge_heads(dk).astype(bf16), qkv_ref[INNER : 2 * INNER, :])
-        grad_xn += dot_nn(merge_heads(dv).astype(bf16), qkv_ref[2 * INNER :, :])
+        grad_xn = dot_nn((merge_heads(dq) * SCALE).astype(bf16), qkv_ref[:INNER, :])
+        grad_xn += dot_nn((merge_heads(dk) * KEY_BACK).astype(bf16), qkv_ref[INNER : 2 * INNER, :])
+        grad_xn += dot_nn(dv, qkv_ref[2 * INNER :, :])
         back = normalize_back(grad_xn, xn_ref[frame].astype(f32), inverse_ref[frame])
         grad_x1 = grad_ref[:, own, :].reshape(patches, width)
         result_ref[frame] = (grad_x1.astype(f32) + back).astype(bf16)
@@ -249,13 +268,16 @@
     allowed = (row_index % GROUP == column_index % GROUP) & (key_valid > 0.5)
     for group in range(groups):
         at = pl.ds(group * rows, rows)
-        q_ref[at, :] = dot_nt(tn_ref[at, :], qkv_ref[:INNER, :]).astype(bf16)
-        k_ref[at, :] = dot_nt(tn_ref[at, :], qkv_ref[INNER : 2 * INNER, :]).astype(bf16)
+        packed = dot_nt(tn_ref[at, :], qkv_ref[: 2 * INNER, :])
+        q_ref[at, :] = (packed[:, :INNER] * QUERY_SCALE).astype(bf16)
+        k_ref[at, :] = packed[:, INNER:].astype(bf16)
+        scores = []
         for head in range(HEADS):
             first, last, _ = window(head)
             query = keep_head(q_ref[at, first:last], head)
-            scores = dot_nt(query, k_ref[at, first:last]) * SCALE
-            raised = jnp.where(allowed, jnp.exp(scores), 0.0)
+            scores.append(dot_nt(query, k_ref[at, first:last]))
+        for head in range(HEADS):
+            raised = jnp.where(allowed, jnp.exp2(scores[head]), 0.0)
             weights = raised * (valid_column / jnp.sum(raised, axis=-1, keepdims=True))
             p_ref[group, head] = weights.astype(bf16)
             c_ref[head : head + 1, at] = jnp.sum(weights, axis=0, keepdims=True)
@@ -369,20 +391,24 @@
     _, valid_column = slot_columns(row_ref[...], count, rows)
     for group in range(groups):
         at = pl.ds(group * rows, rows)
-        dq, dk = [], []
-        for head in range(HEADS):
-            first, last, _ = window(head)
+        grad_scores = []
+        for head in range(HEADS):
             weights = p_ref[group, head].astype(f32)
             along = scores_grad[head : head + 1, group * rows : (group + 1) * rows]
             inner = jnp.sum(weights * along, axis=-1, keepdims=True)
-            grad_scores = (weights * (along - inner) * SCALE).astype(bf16)
-            dq.append(dot_nn(grad_scores, k_ref[at, first:last]))
-            dk.append(dot_tn(grad_scores, q_ref[at, first:last]))
+            grad_scores.append((weights * (along - inner)).astype(bf16))
+        dq, dk = [], []
+        for head in range(HEADS):
+            first, last, _ = window(head)
+            dq.append(dot_nn(grad_scores[head], k_ref[at, first:last]))
+        for head in range(HEADS):
+            first, last, _ = window(head)
+            dk.append(dot_tn(grad_scores[head], q_ref[at, first:last]))
         own = slice(group * rows, (group + 1) * rows)
         weights_c = jnp.concatenate([c_high[:, own], c_high[:, own], c_low[:, own]], axis=0)
         value_rows = jnp.concatenate([high, low, high], axis=0)
-        grad_tn = dot_nn(merge_heads(dq).astype(bf16), qkv_ref[:INNER, :])
-        grad_tn += dot_nn(merge_heads(dk).astype(bf16), qkv_ref[INNER : 2 * INNER, :])
+        grad_tn = dot_nn((merge_heads(dq) * SCALE).astype(bf16), qkv_ref[:INNER, :])
+        grad_tn += dot_nn((merge_heads(dk) * KEY_BACK).astype(bf16), qkv_ref[INNER : 2 * INNER, :])
         dtn_ref[at, :] = grad_tn + dot_tn(weights_c, value_rows)
     chunk = 8
     for start in range(0, slots, chunk):
@@ -441,10 +467,10 @@
         in_specs=[VMEM] * 2,
         out_specs=(VMEM,) * 3,
         compiler_params=params,
-        cost_estimate=cost(1),
+        cost_estimate=cost(30),
         name="spatial_norm",
     )(counts, frames_in)
-    x1, q, k, v, p = pl.pallas_call(
+    x1, q, k, v, p, so = pl.pallas_call(
         spatial_forward,
         out_shape=(
             shape(traded, bf16),
@@ -452,9 +478,10 @@
             shape((local_frames, patches, INNER), bf16),
             shape((local_frames, patches, INNER), bf16),
             shape((local_frames, HEADS, patches, patches), bf16),
+            shape((local_frames, patches, INNER), bf16),
         ),
         in_specs=[VMEM] * 4,
-        out_specs=(VMEM,) * 5,
+        out_specs=(VMEM,) * 6,
         compiler_params=params,
         cost_estimate=cost(8),
         name="spatial_forward",
@@ -520,7 +547,7 @@
     result = pl.pallas_call(
         spatial_backward,
         out_shape=shape(frames_in.shape, bf16),
-        in_specs=[VMEM] * 9,
+        in_specs=[VMEM] * 10,
         out_specs=HBM,
         scratch_shapes=[
             pltpu.VMEM(frames_in.shape, bf16),
@@ -529,7 +556,7 @@
         compiler_params=params,
         cost_estimate=cost(12),
         name="spatial_backward",
-    )(grad_x1, xn, xn_inverse, spatial_qkv, spatial_out, q, k, v, p)
+    )(grad_x1, xn, xn_inverse, spatial_qkv, spatial_out, q, k, v, p, so)
     return (result[None], loss[0, 0])
 
 

time: 117 us -> 110 us (0.940)
  Pallas kernels: 38.2 us -> 33.4 us
  local copies, waits for them, and re-layouts: 5.65 us -> 3.37 us
    pallas_call x1, Pallas kernels: 12.9 us -> 9.6 us  [per_device(): pl.pallas_call(spatial_backward, out_shape=shape(frames_in.shape, bf16),...]
    unnamed x26 -> x18, local copies, waits for them, and re-layouts: 5.65 us -> 3.37 us
where the time goes in v1:
time: 110 us; the launch traced here: 109 us
  blocking collectives  71 us (65%)
  Pallas kernels  33.4 us (30%)
  local copies, waits for them, and re-layouts  3.37 us (3%)
  between operations  1.57 us (1%)
    all_to_all x1, blocking collectives, per_device(): x1 = lax.all_to_all(x1, 'frame', split_axis=0, concat_axis=0, tiled=True)  29 us
    all_to_all x1, blocking collectives, per_device(): lax.all_to_all(grad_x1.reshape(traded), 'frame', split_axis=0, concat_axi...  23.6 us
    all_to_all x1, blocking collectives, per_device(): lax.all_to_all(send, ('batch', 'frame'), split_axis=0, concat_axis=0, til...  18.4 us
    pallas_call x1, Pallas kernels, per_device(): pl.pallas_call(spatial_backward, out_shape=shape(frames_in.shape, bf16),...  9.6 us
    pallas_call x1, Pallas kernels, per_device(): pl.pallas_call(functools.partial(temporal_backward, clips, float(slots *...  8.7 us
    pallas_call x1, Pallas kernels, per_device(): pl.pallas_call(temporal_forward, out_shape=(shape((devices, 1, embed_size...  7.47 us
    pallas_call x1, Pallas kernels, per_device(): pl.pallas_call(spatial_forward, out_shape=(shape(traded, bf16), shape((lo...  6.32 us
    unnamed x18, local copies, waits for them, and re-layouts  3.37 us

profile of v1, /device:TPU:0, one launch (start us, length us, event | category | flops | bytes accessed | tf_op | source)
XLA Modules:
  0.0 109.3 jit_solution(10370547354077379138)
XLA Ops:
  1.3 0.0 copy-start.4
  1.3 1.4 %copy-done.4 = bf16[1,2,256,1408]{3,2,1,0:T(8,128)(2,1)S(1)} copy-done((bf16[1,2,256,1408]{3,2,1,0:T(8,128)(2,1)S(1)}, bf16[1,2,256,1408]{3,2,1,0:T(8,128)(2,1)}, u32[]{:S(2)}) %copy-start.4) | copy-done | bytes 1441816
  2.6 0.0 copy-start.1
  2.6 0.0 copy-start.3
  2.6 1.3 %spatial_norm.1 = (bf16[2,256,1408]{2,1,0:T(8,128)(2,1)S(1)}, f32[2,256,1]{2,1,0:T(8,128)S(1)}, s32[1,1]{1,0:T(1,128)}) custom-call(s32[1,1]{1,0:T(1,128)} %bitcast.8.count_ref, bf16[2,256,1408]{2,1,0:T(8,128)(2,1)S(1)} %bitcast.15), custom_call_target="tpu_custom_call" | custom-call | flops 30000001024 | tf_op jit(solution)/shard_map/spatial_norm/pallas_call | solution.py:460
  3.9 1.4 %copy-done.1 = bf16[1408,2112]{0,1:T(8,128)(2,1)S(1)} copy-done((bf16[1408,2112]{0,1:T(8,128)(2,1)S(1)}, bf16[1408,2112]{0,1:T(8,128)(2,1)}, u32[]{:S(2)}) %copy-start.1) | copy-done | bytes 5947416
  5.3 0.6 copy-done.3
  5.9 0.0 copy-start
  5.9 0.0 copy-start.5
  5.9 6.3 %spatial_forward.1 = (bf16[16,32,1408]{2,1,0:T(8,128)(2,1)S(1)}, bf16[2,256,704]{2,1,0:T(8,128)(2,1)S(1)}, bf16[2,256,704]{2,1,0:T(8,128)(2,1)S(1)}, bf16[2,256,...) custom-call(bf16[2,256,1408]{2,1,0:T(8,128)(2,1)S(1)} %bitcast.16, ...), custom_call_target="tpu_custom_call" | custom-call | flops 8000000000 | tf_op jit(solution)/shard_map/spatial_forward/pallas_call | solution.py:473
  12.3 0.0 copy-start.2
  12.3 0.0 copy-start.6
  12.3 0.0 copy-start.7
  12.3 0.0 copy-start.8
  12.3 29.0 %all_to_all.15 = bf16[16,32,1408]{2,1,0:T(8,128)(2,1)S(1)} all-to-all(bf16[16,32,1408]{2,1,0:T(8,128)(2,1)S(1)} %get-tuple-element.22), channel_id=1, replica_groups=mesh['batch'=8,'frame'=16] {'frame'}, dimensions={0} | all-to-all | bytes 2883584 | tf_op jit(solution)/shard_map/all_to_all | solution.py:490
  41.3 0.0 copy-done
  41.3 0.0 copy-done.5
  41.3 0.0 copy-done.2
  41.3 0.0 copy-done.6
  41.3 0.0 copy-done.7
  41.3 0.0 copy-done.8
  41.3 7.5 %temporal_forward.1 = (f32[128,1,640]{2,1,0:T(1,128)S(1)}, bf16[512,1408]{1,0:T(8,128)(2,1)S(1)}, f32[512,1]{1,0:T(8,128)S(1)}, bf16[512,704]{1,0:T(8,128)(2,1)S...) custom-call(s32[1,1]{1,0:T(1,128)} %get-tuple-element.20.count_ref, ...), custom_call_target="tpu_custom_call" | custom-call | flops 7000000000 | tf_op jit(solution)/shard_map/temporal_forward/pallas_call | solution.py:493
  48.8 18.4 %all_to_all.16.parts_ref = f32[128,1,640]{2,1,0:T(1,128)S(1)} all-to-all(f32[128,1,640]{2,1,0:T(1,128)S(1)} %get-tuple-element.23), channel_id=1, replica_groups=mesh['batch'=8,'frame'=16] {'batch','frame'}, dimensions={0} | all-to-all | bytes 655360 | tf_op jit(solution)/shard_map/all_to_all | solution.py:520
  67.2 8.7 %temporal_backward.1 = (bf16[32,16,1408]{2,1,0:T(8,128)(2,1)S(1)}, f32[1,1]{1,0:T(1,128)}) custom-call(s32[1,1]{1,0:T(1,128)} %get-tuple-element.20.count_ref, s32[1,32]{1,0:T(1,128)S(1)} %copy-done.8, f32[128,1,640]{2,1,0:T(1,128)S(1)} %all_to_all.16.parts_ref, bf16[512,1408]{1,0:T(8,128)(2,1)S(1)} %get-tuple-element.24.tn_ref, ...), custom_call_target="tpu_custom_call" | custom-call | flops 8000000000 | tf_op jit(solution)/shard_map/temporal_backward/pallas_call | solution.py:521
  75.9 23.6 %all_to_all.17.grad_ref = bf16[16,32,1408]{2,1,0:T(8,128)(2,1)S(1)} all-to-all(bf16[16,32,1408]{2,1,0:T(8,128)(2,1)S(1)} %bitcast.9), channel_id=1, replica_groups=mesh['batch'=8,'frame'=16] {'frame'}, dimensions={0} | all-to-all | bytes 2883584 | tf_op jit(solution)/shard_map/all_to_all | solution.py:544
  99.5 9.6 %spatial_backward.1 = bf16[2,256,1408]{2,1,0:T(8,128)(2,1)} custom-call(bf16[16,32,1408]{2,1,0:T(8,128)(2,1)S(1)} %all_to_all.17.grad_ref, bf16[2,256,1408]{2,1,0:T(8,128)(2,1)S(1)} %get-tuple-element.21.xn_ref, f32[2,256,1]{2,1,0:T(8,128)S(1)} %get-tuple-element.31.inverse_ref, bf16[2112,1408]{1,0:T(8,128)(2,1)S(1)} %bitcast.14, ...), custom_call_target="tpu_custom_call" | custom-call | flops 12000000000 | tf_op jit(solution)/shard_map/spatial_backward/pallas_call | solution.py:547
Async XLA Ops:
  1.3 1.4 %copy-start.4 = (bf16[1,2,256,1408]{3,2,1,0:T(8,128)(2,1)S(1)}, bf16[1,2,256,1408]{3,2,1,0:T(8,128)(2,1)}, u32[]{:S(2)}) copy-start(bf16[1,2,256,1408]{3,2,1,0:T(8,128)(2,1)} %param.10) | copy-start | bytes 4325380
  2.6 2.7 %copy-start.1 = (bf16[1408,2112]{0,1:T(8,128)(2,1)S(1)}, bf16[1408,2112]{0,1:T(8,128)(2,1)}, u32[]{:S(2)}) copy-start(bf16[1408,2112]{0,1:T(8,128)(2,1)} %param.13) | copy-start | bytes 17842180
  2.6 3.3 %copy-start.3 = (bf16[704,1408]{1,0:T(8,128)(2,1)S(1)}, bf16[704,1408]{1,0:T(8,128)(2,1)}, u32[]{:S(2)}) copy-start(bf16[704,1408]{1,0:T(8,128)(2,1)} %out_ref.7) | copy-start | bytes 5947396
  5.9 35.3 %copy-start = (bf16[1408,2112]{0,1:T(8,128)(2,1)S(1)}, bf16[1408,2112]{0,1:T(8,128)(2,1)}, u32[]{:S(2)}) copy-start(bf16[1408,2112]{0,1:T(8,128)(2,1)} %param.15) | copy-start | bytes 17842180
  5.9 35.3 %copy-start.5 = (bf16[1408,512]{1,0:T(8,128)(2,1)S(1)}, bf16[1408,512]{1,0:T(8,128)(2,1)}, u32[]{:S(2)}) copy-start(bf16[1408,512]{1,0:T(8,128)(2,1)} %proj_ref.3) | copy-start | bytes 4325380
  12.3 29.0 %copy-start.2 = (bf16[704,1408]{1,0:T(8,128)(2,1)S(1)}, bf16[704,1408]{1,0:T(8,128)(2,1)}, u32[]{:S(2)}) copy-start(bf16[704,1408]{1,0:T(8,128)(2,1)} %out_ref.6) | copy-start | bytes 5947396
  12.3 29.0 %copy-start.6 = (f32[32,1408]{1,0:T(8,128)S(1)}, f32[32,1408]{1,0:T(8,128)}, u32[]{:S(2)}) copy-start(f32[32,1408]{1,0:T(8,128)} %embed_ref.1) | copy-start | bytes 540676
  12.3 29.0 %copy-start.7 = (f32[1,512]{1,0:T(1,128)S(1)}, f32[1,512]{1,0:T(1,128)}, u32[]{:S(2)}) copy-start(f32[1,512]{1,0:T(1,128)} %text_ref.1) | copy-start | bytes 6148
  12.3 29.0 %copy-start.8 = (s32[1,32]{1,0:T(1,128)S(1)}, s32[1,32]{1,0:T(1,128)}, u32[]{:S(2)}) copy-start(s32[1,32]{1,0:T(1,128)} %row_ref.3) | copy-start | bytes 388

commit v2 on v1

--- a/solution.py
+++ b/solution.py
@@ -13,6 +13,7 @@
 INNER = HEADS * HD
 LANES = 128
 GROUP = 8
+PIECES = 4
 EPSILON = 1e-06
 SHARPNESS = 1.0 / 0.07
 SCALE = 1.0 / math.sqrt(HD)
@@ -48,7 +49,7 @@
     return parts
 
 
-def exact(dot, values, matrix, terms=3):
+def exact(dot, values, matrix, terms=2):
     rows = values.shape[0]
     products = dot(jnp.concatenate(split_terms(values, terms), axis=0), matrix)
     total = products[:rows]
@@ -106,21 +107,19 @@
     )
 
 
-def spatial_norm(count_ref, tok_ref, xn_ref, inverse_ref, count_out_ref):
-    count_out_ref[...] = count_ref[...]
+def spatial_norm(count_ref, tok_ref, xn_ref, inverse_ref, info_ref):
+    count = count_ref[...].astype(f32)
+    info_ref[0:1, :] = jnp.broadcast_to(count, (1, info_ref.shape[1]))
+    scale = 1.0 / (count * float(tok_ref.shape[1]))
+    info_ref[1:2, :] = jnp.broadcast_to(scale, (1, info_ref.shape[1]))
     for frame in range(tok_ref.shape[0]):
         normed, inverse = normalize(tok_ref[frame].astype(f32))
         xn_ref[frame] = normed.astype(bf16)
         inverse_ref[frame] = inverse
 
 
-def spatial_forward(
-    tok_ref, xn_ref, qkv_ref, out_ref, x1_ref, q_ref, k_ref, v_ref, p_ref, so_ref
-):
-    frames, patches, _ = tok_ref.shape
-    owners = x1_ref.shape[0]
-    share = patches // owners
-    for frame in range(frames):
+def spatial_attention(xn_ref, qkv_ref, q_ref, k_ref, v_ref, p_ref, so_ref):
+    for frame in range(xn_ref.shape[0]):
         packed = dot_nt(xn_ref[frame], qkv_ref[...])
         q_ref[frame] = (packed[:, :INNER] * QUERY_SCALE).astype(bf16)
         k_ref[frame] = packed[:, INNER : 2 * INNER].astype(bf16)
@@ -139,10 +138,17 @@
             first, last, _ = window(head)
             mixed.append(dot_nn(p_ref[frame, head], v_ref[frame, :, first:last]))
         so_ref[frame] = merge_heads(mixed).astype(bf16)
+
+
+def spatial_output(tok_ref, so_ref, out_ref, x1_ref):
+    frames, patches, width = tok_ref.shape
+    owners = x1_ref.shape[0]
+    share = patches // owners
+    for frame in range(frames):
         update = dot_nn(so_ref[frame], out_ref[...])
         x1 = (tok_ref[frame].astype(f32) + update).astype(bf16)
         own = slice(frame * share, (frame + 1) * share)
-        x1_ref[:, own, :] = x1.reshape(owners, share, x1.shape[-1])
+        x1_ref[:, own, :] = x1.reshape(owners, share, width)
 
 
 def spatial_backward(
@@ -156,10 +162,17 @@
     v_ref,
     p_ref,
     so_ref,
+    loss_ref,
     result_hbm,
+    loss_hbm,
     result_ref,
+    loss_held_ref,
     result_sem,
+    loss_sem,
 ):
+    loss_held_ref[...] = loss_ref[:1, :1]
+    loss_copy = pltpu.make_async_copy(loss_held_ref, loss_hbm, loss_sem)
+    loss_copy.start()
     frames, patches, width = xn_ref.shape
     owners = grad_ref.shape[0]
     share = patches // owners
@@ -190,30 +203,38 @@
         grad_xn = dot_nn((merge_heads(dq) * SCALE).astype(bf16), qkv_ref[:INNER, :])
         grad_xn += dot_nn((merge_heads(dk) * KEY_BACK).astype(bf16), qkv_ref[INNER : 2 * INNER, :])
         grad_xn += dot_nn(dv, qkv_ref[2 * INNER :, :])
-        back = normalize_back(grad_xn, xn_ref[frame].astype(f32), inverse_ref[frame])
-        grad_x1 = grad_ref[:, own, :].reshape(patches, width)
-        result_ref[frame] = (grad_x1.astype(f32) + back).astype(bf16)
-        copy = pltpu.make_async_copy(
-            result_ref.at[frame], result_hbm.at[frame], result_sem.at[frame]
-        )
-        copy.start()
-        copies.append(copy)
-    for copy in copies:
+        for piece in range(PIECES):
+            size = patches // PIECES
+            at = slice(piece * size, (piece + 1) * size)
+            back = normalize_back(
+                grad_xn[at], xn_ref[frame, at].astype(f32), inverse_ref[frame, at]
+            )
+            held = slice(piece * owners // PIECES, (piece + 1) * owners // PIECES)
+            grad_x1 = grad_ref[held, own, :].reshape(size, width)
+            result_ref[frame, at] = (grad_x1.astype(f32) + back).astype(bf16)
+            rows = pl.ds(piece * size, size)
+            copy = pltpu.make_async_copy(
+                result_ref.at[frame, rows],
+                result_hbm.at[frame, rows],
+                result_sem.at[frame, piece],
+            )
+            copy.start()
+            copies.append(copy)
+    for copy in copies + [loss_copy]:
         copy.wait()
 
 
-def slot_columns(times_row, count, rows):
-    slots = times_row.shape[1]
-    valid = jnp.where(times_row < count, 1.0, 0.0).astype(f32)
+def slot_columns(valid, rows):
+    slots = valid.shape[1]
     row_slot = lax.broadcasted_iota(jnp.int32, (rows, slots), 0) // GROUP
     slot = lax.broadcasted_iota(jnp.int32, (rows, slots), 1)
     column = jnp.sum(jnp.where(row_slot == slot, valid, 0.0), axis=1, keepdims=True)
-    return valid, column
+    return column
 
 
 def temporal_forward(
-    count_ref,
-    row_ref,
+    info_ref,
+    times_ref,
     x1_ref,
     embed_ref,
     qkv_ref,
@@ -231,25 +252,31 @@
     slots, share, width = x1_ref.shape
     groups = share // GROUP
     rows = slots * GROUP
-    count = count_ref[...]
-    lookup = jnp.where(
-        lax.broadcasted_iota(jnp.int32, (embed_ref.shape[0], slots), 0) == row_ref[...], 1.0, 0.0
-    ).astype(bf16)
+    times = times_ref[...].astype(f32)
+    valid = jnp.where(times < info_ref[0:1, :slots], 1.0, 0.0)
+    time = lax.broadcasted_iota(jnp.int32, (embed_ref.shape[0], slots), 0).astype(f32)
+    lookup = jnp.where(time == times, 1.0, 0.0).astype(bf16)
     added = None
     for part in split_terms(embed_ref[...], 3):
         term = dot_tn(lookup, part)
         added = term if added is None else added + term
-    valid, valid_column = slot_columns(row_ref[...], count, rows)
+    valid_column = slot_columns(valid, rows)
+    slot_index = lax.broadcasted_iota(jnp.int32, (slots, slots), 0)
+    own_slot = slot_index == lax.broadcasted_iota(jnp.int32, (slots, slots), 1)
+    valid_slots = jnp.sum(jnp.where(own_slot, valid, 0.0), axis=1, keepdims=True)
     chunk = 8
-    pooled = jnp.zeros((1, width), f32)
+    all_rows = slots * share
+    row_slot = lax.broadcasted_iota(jnp.int32, (slots, all_rows), 1) // share
+    own_row = lax.broadcasted_iota(jnp.int32, (slots, all_rows), 0) == row_slot
+    spread_rows = jnp.where(own_row, 1.0, 0.0).astype(bf16)
+    valid_rows = jnp.broadcast_to(valid, (GROUP, slots)).astype(bf16)
+    row_valid = dot_nn(valid_rows, spread_rows).astype(bf16)
+    pooled = dot_nn(row_valid, x1_ref[...].reshape(all_rows, width))[:1]
+    for slot in range(0, slots, GROUP):
+        kept = valid_slots[slot : slot + GROUP] * added[slot : slot + GROUP]
+        pooled = pooled + float(share) * jnp.sum(kept, axis=0, keepdims=True)
     for start in range(0, slots, chunk):
         y = x1_ref[start : start + chunk].astype(f32) + added[start : start + chunk][:, None, :]
-        part = jnp.sum(y, axis=1)
-        slot_valid = jnp.concatenate(
-            [valid_column[(start + i) * GROUP : (start + i) * GROUP + 1] for i in range(chunk)],
-            axis=0,
-        )
-        pooled = pooled + jnp.sum(part * slot_valid, axis=0, keepdims=True)
         normed, inverse = normalize(y)
         for group in range(groups):
             own = slice(group * GROUP, (group + 1) * GROUP)
@@ -281,7 +308,7 @@
             weights = raised * (valid_column / jnp.sum(raised, axis=-1, keepdims=True))
             p_ref[group, head] = weights.astype(bf16)
             c_ref[head : head + 1, at] = jnp.sum(weights, axis=0, keepdims=True)
-    gathered = exact(dot_nn, c_ref[...], tn_ref[...], 2)
+    gathered = exact(dot_nn, c_ref[...], tn_ref[...])
     mixed_all = exact(dot_nt, gathered, qkv_ref[2 * INNER :, :])
     lane = lax.broadcasted_iota(jnp.int32, mixed_all.shape, 1)
     head_row = lax.broadcasted_iota(jnp.int32, mixed_all.shape, 0)
@@ -289,7 +316,7 @@
     mixed = jnp.sum(jnp.where(own_lane, mixed_all, 0.0), axis=0, keepdims=True)
     feature = pooled + exact(dot_nn, jnp.broadcast_to(mixed, (GROUP, INNER)), out_ref[...])[:1]
     z = exact(dot_nn, jnp.broadcast_to(feature, (GROUP, width)), proj_ref[...])[:1]
-    z = z / (count.astype(f32) * float(PATCHES))
+    z = z * info_ref[1:2, :1]
     embed_size = z.shape[1]
     send_ref[:, :, :embed_size] = jnp.broadcast_to(
         z[None], (send_ref.shape[0], 1, embed_size)
@@ -303,9 +330,6 @@
     send_ref[:, :, embed_size:] = jnp.broadcast_to(piece[None], (send_ref.shape[0], 1, LANES))
 
 
-PATCHES = 256
-
-
 def unit_rows(matrix):
     inverse = lax.rsqrt(jnp.sum(matrix * matrix, axis=-1, keepdims=True) + EPSILON)
     return matrix * inverse, inverse
@@ -314,8 +338,8 @@
 def temporal_backward(
     batch,
     cotangent,
-    count_ref,
-    row_ref,
+    info_ref,
+    times_ref,
     parts_ref,
     tn_ref,
     inverse_ref,
@@ -333,15 +357,14 @@
     slots, share, width = grad_ref.shape
     groups = share // GROUP
     rows = slots * GROUP
-    count = count_ref[...]
     clips = batch
     per_clip = parts_ref.shape[0] // clips
     embed_size = proj_ref.shape[1]
-    parts = parts_ref[:, 0, :].reshape(clips, per_clip, parts_ref.shape[2])
-    z = jnp.sum(parts[:, :, :embed_size], axis=1)
+    parts = parts_ref[:, 0, :].reshape(per_clip, clips, parts_ref.shape[2])
+    z = jnp.sum(parts[:, :, :embed_size], axis=0)
     tiles = embed_size // LANES
     text = jnp.concatenate(
-        [parts[:, i * (per_clip // tiles), embed_size:] for i in range(tiles)], axis=1
+        [parts[i * (per_clip // tiles), :, embed_size:] for i in range(tiles)], axis=1
     )
     e, inverse_z = unit_rows(z)
     u, _ = unit_rows(text)
@@ -366,7 +389,7 @@
         + 0.5 * jnp.sum(jnp.log(column_total), axis=1, keepdims=True)
         - jnp.sum(jnp.sum(jnp.where(diagonal, logits, 0.0), axis=1, keepdims=True), axis=0, keepdims=True)
     )
-    loss_ref[...] = loss
+    loss_ref[...] = jnp.broadcast_to(loss, loss_ref.shape)
     shares = 0.5 * (raised / row_total + raised / column_total) - jnp.where(diagonal, 1.0, 0.0)
     grad_e = (cotangent * SHARPNESS) * lax.dot_general(
         shares,
@@ -378,7 +401,7 @@
     grad_z = inverse_z * (grad_e - e * jnp.sum(e * grad_e, axis=-1, keepdims=True))
     own = lax.broadcasted_iota(jnp.int32, grad_z.shape, 0) == lax.axis_index("batch")
     grad_own = jnp.sum(jnp.where(own, grad_z, 0.0), axis=0, keepdims=True)
-    grad_own = grad_own / (count.astype(f32) * float(PATCHES))
+    grad_own = grad_own * info_ref[1:2, :1]
     grad_feature = exact(dot_nt, jnp.broadcast_to(grad_own, grad_z.shape), proj_ref[...])
     grad_mixed = exact(dot_nt, grad_feature, out_ref[...])
     lane = lax.broadcasted_iota(jnp.int32, grad_mixed.shape, 1)
@@ -386,9 +409,11 @@
     own_lane = (lane >= head_row * HD) & (lane < head_row * HD + HD)
     value_grad = exact(dot_nn, jnp.where(own_lane, grad_mixed, 0.0), qkv_ref[2 * INNER :, :])
     high, low = split_terms(value_grad, 2)
-    scores_grad = exact(dot_nt, value_grad, tn_ref[...], 2)
+    scores_grad = exact(dot_nt, value_grad, tn_ref[...])
     c_high, c_low = split_terms(c_ref[...], 2)
-    _, valid_column = slot_columns(row_ref[...], count, rows)
+    times = times_ref[...].astype(f32)
+    valid = jnp.where(times < info_ref[0:1, :slots], 1.0, 0.0)
+    valid_column = slot_columns(valid, rows)
     for group in range(groups):
         at = pl.ds(group * rows, rows)
         grad_scores = []
@@ -455,37 +480,44 @@
     params = pltpu.CompilerParams(vmem_limit_bytes=20 * MIB)
     spatial_qkv = spatial_qkv.T
     temporal_qkv = temporal_qkv.T
-    counts = valid_count.reshape(1, 1)
-
-    xn, xn_inverse, counts = pl.pallas_call(
+    xn, xn_inverse, info = pl.pallas_call(
         spatial_norm,
         out_shape=(
             shape(frames_in.shape, bf16),
             shape((local_frames, patches, 1), f32),
-            shape((1, 1), jnp.int32),
+            shape((GROUP, LANES), f32),
         ),
         in_specs=[VMEM] * 2,
         out_specs=(VMEM,) * 3,
         compiler_params=params,
         cost_estimate=cost(30),
         name="spatial_norm",
-    )(counts, frames_in)
-    x1, q, k, v, p, so = pl.pallas_call(
-        spatial_forward,
+    )(valid_count.reshape(1, 1), frames_in)
+    part = shape((local_frames, patches, INNER), bf16)
+    q, k, v, p, so = pl.pallas_call(
+        spatial_attention,
         out_shape=(
-            shape(traded, bf16),
-            shape((local_frames, patches, INNER), bf16),
-            shape((local_frames, patches, INNER), bf16),
-            shape((local_frames, patches, INNER), bf16),
+            part,
+            part,
+            part,
             shape((local_frames, HEADS, patches, patches), bf16),
-            shape((local_frames, patches, INNER), bf16),
+            part,
         ),
-        in_specs=[VMEM] * 4,
-        out_specs=(VMEM,) * 6,
+        in_specs=[VMEM] * 2,
+        out_specs=(VMEM,) * 5,
         compiler_params=params,
         cost_estimate=cost(8),
-        name="spatial_forward",
-    )(frames_in, xn, spatial_qkv, spatial_out)
+        name="spatial_attention",
+    )(xn, spatial_qkv)
+    x1 = pl.pallas_call(
+        spatial_output,
+        out_shape=shape(traded, bf16),
+        in_specs=[VMEM] * 3,
+        out_specs=VMEM,
+        compiler_params=params,
+        cost_estimate=cost(2),
+        name="spatial_output",
+    )(frames_in, so, spatial_out)
 
     x1 = lax.all_to_all(x1, "frame", split_axis=0, concat_axis=0, tiled=True)
     x1 = x1.reshape(slots, share, width)
@@ -507,7 +539,7 @@
         cost_estimate=cost(7),
         name="temporal_forward",
     )(
-        counts,
+        info,
         frame_time,
         x1,
         time_embed,
@@ -517,10 +549,10 @@
         text_embed,
     )
 
-    parts = lax.all_to_all(send, ("batch", "frame"), split_axis=0, concat_axis=0, tiled=True)
+    parts = lax.all_to_all(send, ("frame", "batch"), split_axis=0, concat_axis=0, tiled=True)
     grad_x1, loss = pl.pallas_call(
         functools.partial(temporal_backward, clips, float(slots * patches)),
-        out_shape=(shape((slots, share, width), bf16), shape((1, 1), f32)),
+        out_shape=(shape((slots, share, width), bf16), shape((GROUP, LANES), f32)),
         in_specs=[VMEM] * 12,
         out_specs=(VMEM,) * 2,
         scratch_shapes=[pltpu.VMEM((rows, width), f32)],
@@ -528,7 +560,7 @@
         cost_estimate=cost(8),
         name="temporal_backward",
     )(
-        counts,
+        info,
         frame_time,
         parts,
         tn,
@@ -544,19 +576,21 @@
     grad_x1 = lax.all_to_all(
         grad_x1.reshape(traded), "frame", split_axis=0, concat_axis=0, tiled=True
     )
-    result = pl.pallas_call(
+    result, loss = pl.pallas_call(
         spatial_backward,
-        out_shape=shape(frames_in.shape, bf16),
-        in_specs=[VMEM] * 10,
-        out_specs=HBM,
+        out_shape=(shape(frames_in.shape, bf16), shape((1, 1), f32)),
+        in_specs=[VMEM] * 11,
+        out_specs=(HBM, HBM),
         scratch_shapes=[
             pltpu.VMEM(frames_in.shape, bf16),
-            pltpu.SemaphoreType.DMA((local_frames,)),
+            pltpu.VMEM((1, 1), f32),
+            pltpu.SemaphoreType.DMA((local_frames, PIECES)),
+            pltpu.SemaphoreType.DMA,
         ],
         compiler_params=params,
         cost_estimate=cost(12),
         name="spatial_backward",
-    )(grad_x1, xn, xn_inverse, spatial_qkv, spatial_out, q, k, v, p, so)
+    )(grad_x1, xn, xn_inverse, spatial_qkv, spatial_out, q, k, v, p, so, loss)
     return (result[None], loss[0, 0])
 
 

time: 110 us -> 109 us (level)
  Pallas kernels: 33.4 us -> 31.9 us
    pallas_call x2 -> x3, Pallas kernels: 15.9 us -> 16.3 us  [the longest x1 9.74 us: per_device(): pl.pallas_call(spatial_backward, out_shape=(shape(frames_in.shape, bf16),...]
    unnamed x18 -> x20, local copies, waits for them, and re-layouts: 3.37 us -> 3.22 us
where the time goes in v2:
time: 109 us
  blocking collectives  71.8 us (66%)
  Pallas kernels  31.9 us (29%)
  local copies, waits for them, and re-layouts  3.22 us (3%)
  between operations  1.61 us (1%)
    all_to_all x1, blocking collectives, per_device(): x1 = lax.all_to_all(x1, 'frame', split_axis=0, concat_axis=0, tiled=True)  29.1 us
    all_to_all x1, blocking collectives, per_device(): lax.all_to_all(grad_x1.reshape(traded), 'frame', split_axis=0, concat_axi...  24.4 us
    all_to_all x1, blocking collectives, per_device(): lax.all_to_all(send, ('frame', 'batch'), split_axis=0, concat_axis=0, til...  18.3 us
    pallas_call x1, Pallas kernels, per_device(): pl.pallas_call(spatial_backward, out_shape=(shape(frames_in.shape, bf16),...  9.74 us
    pallas_call x1, Pallas kernels, per_device(): pl.pallas_call(functools.partial(temporal_backward, clips, float(slots *...  7.92 us
    pallas_call x1, Pallas kernels, per_device(): pl.pallas_call(temporal_forward, out_shape=(shape((devices, 1, embed_size...  6.85 us
    pallas_call x1, Pallas kernels, per_device(): pl.pallas_call(spatial_attention, out_shape=(part, part, part, shape((loc...  5.11 us
    unnamed x20, local copies, waits for them, and re-layouts  3.22 us

profile of v2, /device:TPU:0, one launch (start us, length us, event | category | flops | bytes accessed | tf_op | source)
XLA Modules:
  0.0 108.5 jit_solution(2972359796584879310)
XLA Ops:
  1.3 0.0 copy-start.4
  1.3 1.4 %copy-done.4 = bf16[1,2,256,1408]{3,2,1,0:T(8,128)(2,1)S(1)} copy-done((bf16[1,2,256,1408]{3,2,1,0:T(8,128)(2,1)S(1)}, bf16[1,2,256,1408]{3,2,1,0:T(8,128)(2,1)}, u32[]{:S(2)}) %copy-start.4) | copy-done | bytes 1441816
  2.6 0.0 copy-start.1
  2.6 0.9 spatial_norm.1
  3.5 1.8 %copy-done.1 = bf16[1408,2112]{0,1:T(8,128)(2,1)S(1)} copy-done((bf16[1408,2112]{0,1:T(8,128)(2,1)S(1)}, bf16[1408,2112]{0,1:T(8,128)(2,1)}, u32[]{:S(2)}) %copy-start.1) | copy-done | bytes 5947416
  5.3 0.0 copy-start.3
  5.3 0.0 copy-start.5
  5.3 5.1 %spatial_attention.1 = (bf16[2,256,704]{2,1,0:T(8,128)(2,1)S(1)}, bf16[2,256,704]{2,1,0:T(8,128)(2,1)S(1)}, bf16[2,256,704]{2,1,0:T(8,128)(2,1)S(1)}, bf16[2,8,2...) custom-call(bf16[2,256,1408]{2,1,0:T(8,128)(2,1)S(1)} %get-tuple-element.22.xn_ref, bf16[2112,1408]{1,0:T(8,128)(2,1)S(1)} %bitcast.13), custom_call_target="tpu_custom_call" | custom-call | flops 8000000000 | tf_op jit(solution)/shard_map/spatial_attention/pallas_call | solution.py:497
  10.5 0.0 copy-done.3
  10.5 0.0 copy-done.5
  10.5 0.0 copy-start
  10.5 0.0 copy-start.6
  10.5 1.4 %spatial_output.1 = bf16[16,32,1408]{2,1,0:T(8,128)(2,1)S(1)} custom-call(bf16[2,256,1408]{2,1,0:T(8,128)(2,1)S(1)} %bitcast.16, bf16[2,256,704]{2,1,0:T(8,128)(2,1)S(1)} %get-tuple-element.23.so_ref, bf16[704,1408]{1,0:T(8,128)(2,1)S(1)} %copy-done.3), custom_call_target="tpu_custom_call" | custom-call | flops 2000000000 | tf_op jit(solution)/shard_map/spatial_output/pallas_call | solution.py:512
  11.9 0.0 copy-start.2
  11.9 0.0 copy-start.7
  11.9 0.0 copy-start.8
  11.9 0.0 copy-start.9
  12.0 29.1 %all_to_all.15 = bf16[16,32,1408]{2,1,0:T(8,128)(2,1)S(1)} all-to-all(bf16[16,32,1408]{2,1,0:T(8,128)(2,1)S(1)} %spatial_output.1), channel_id=1, replica_groups=mesh['batch'=8,'frame'=16] {'frame'}, dimensions={0} | all-to-all | bytes 2883584 | tf_op jit(solution)/shard_map/all_to_all | solution.py:522
  41.0 0.0 copy-done
  41.0 0.0 copy-done.6
  41.0 0.0 copy-done.2
  41.1 0.0 copy-done.7
  41.1 0.0 copy-done.8
  41.1 0.0 copy-done.9
  41.1 6.9 %temporal_forward.1 = (f32[128,1,640]{2,1,0:T(1,128)S(1)}, bf16[512,1408]{1,0:T(8,128)(2,1)S(1)}, f32[512,1]{1,0:T(8,128)S(1)}, bf16[512,704]{1,0:T(8,128)(2,1)S...) custom-call(f32[8,128]{1,0:T(8,128)S(1)} %get-tuple-element.21.info_ref, ...), custom_call_target="tpu_custom_call" | custom-call | flops 7000000000 | tf_op jit(solution)/shard_map/temporal_forward/pallas_call | solution.py:525
  47.9 18.3 %all_to_all.16.parts_ref = f32[128,1,640]{2,1,0:T(1,128)S(1)} all-to-all(f32[128,1,640]{2,1,0:T(1,128)S(1)} %get-tuple-element.24), channel_id=1, replica_groups=mesh['batch'=8,'frame'=16] {'frame','batch'}, dimensions={0} | all-to-all | bytes 655360 | tf_op jit(solution)/shard_map/all_to_all | solution.py:552
  66.2 7.9 %temporal_backward.1 = (bf16[32,16,1408]{2,1,0:T(8,128)(2,1)S(1)}, f32[8,128]{1,0:T(8,128)S(1)}) custom-call(f32[8,128]{1,0:T(8,128)S(1)} %get-tuple-element.21.info_ref, s32[1,32]{1,0:T(1,128)S(1)} %copy-done.9, f32[128,1,640]{2,1,0:T(1,128)S(1)} %all_to_all.16.parts_ref, bf16[512,1408]{1,0:T(8,128)(2,1)S(1)} %get-tuple-element.25.tn_ref, ...), custom_call_target="tpu_custom_call" | custom-call | flops 8000000000 | tf_op jit(solution)/shard_map/temporal_backward/pallas_call | solution.py:553
  74.2 24.4 %all_to_all.17.grad_ref = bf16[16,32,1408]{2,1,0:T(8,128)(2,1)S(1)} all-to-all(bf16[16,32,1408]{2,1,0:T(8,128)(2,1)S(1)} %bitcast.9), channel_id=1, replica_groups=mesh['batch'=8,'frame'=16] {'frame'}, dimensions={0} | all-to-all | bytes 2883584 | tf_op jit(solution)/shard_map/all_to_all | solution.py:576
  98.6 9.7 %spatial_backward.1 = (bf16[2,256,1408]{2,1,0:T(8,128)(2,1)}, f32[1,1]{1,0:T(1,128)}) custom-call(bf16[16,32,1408]{2,1,0:T(8,128)(2,1)S(1)} %all_to_all.17.grad_ref, bf16[2,256,1408]{2,1,0:T(8,128)(2,1)S(1)} %get-tuple-element.22.xn_ref, f32[2,256,1]{2,1,0:T(8,128)S(1)} %get-tuple-element.32.inverse_ref, bf16[2112,1408]{1,0:T(8,128)(2,1)S(1)} %bitcast.14, ...), custom_call_target="tpu_custom_call" | custom-call | flops 12000000000 | tf_op jit(solution)/shard_map/spatial_backward/pallas_call | solution.py:579
Async XLA Ops:
  1.3 1.4 %copy-start.4 = (bf16[1,2,256,1408]{3,2,1,0:T(8,128)(2,1)S(1)}, bf16[1,2,256,1408]{3,2,1,0:T(8,128)(2,1)}, u32[]{:S(2)}) copy-start(bf16[1,2,256,1408]{3,2,1,0:T(8,128)(2,1)} %param.10) | copy-start | bytes 4325380
  2.6 2.7 %copy-start.1 = (bf16[1408,2112]{0,1:T(8,128)(2,1)S(1)}, bf16[1408,2112]{0,1:T(8,128)(2,1)}, u32[]{:S(2)}) copy-start(bf16[1408,2112]{0,1:T(8,128)(2,1)} %param.13) | copy-start | bytes 17842180
  5.3 5.1 %copy-start.3 = (bf16[704,1408]{1,0:T(8,128)(2,1)S(1)}, bf16[704,1408]{1,0:T(8,128)(2,1)}, u32[]{:S(2)}) copy-start(bf16[704,1408]{1,0:T(8,128)(2,1)} %out_ref.7) | copy-start | bytes 5947396
  5.3 5.1 %copy-start.5 = (bf16[1,2,256,1408]{3,2,1,0:T(8,128)(2,1)S(1)}, bf16[1,2,256,1408]{3,2,1,0:T(8,128)(2,1)}, u32[]{:S(2)}) copy-start(bf16[1,2,256,1408]{3,2,1,0:T(8,128)(2,1)} %param.10) | copy-start | bytes 4325380
  10.5 30.6 %copy-start = (bf16[1408,2112]{0,1:T(8,128)(2,1)S(1)}, bf16[1408,2112]{0,1:T(8,128)(2,1)}, u32[]{:S(2)}) copy-start(bf16[1408,2112]{0,1:T(8,128)(2,1)} %param.15) | copy-start | bytes 17842180
  10.5 30.6 %copy-start.6 = (bf16[1408,512]{1,0:T(8,128)(2,1)S(1)}, bf16[1408,512]{1,0:T(8,128)(2,1)}, u32[]{:S(2)}) copy-start(bf16[1408,512]{1,0:T(8,128)(2,1)} %proj_ref.3) | copy-start | bytes 4325380
  11.9 29.1 %copy-start.2 = (bf16[704,1408]{1,0:T(8,128)(2,1)S(1)}, bf16[704,1408]{1,0:T(8,128)(2,1)}, u32[]{:S(2)}) copy-start(bf16[704,1408]{1,0:T(8,128)(2,1)} %out_ref.6) | copy-start | bytes 5947396
  11.9 29.1 %copy-start.7 = (f32[32,1408]{1,0:T(8,128)S(1)}, f32[32,1408]{1,0:T(8,128)}, u32[]{:S(2)}) copy-start(f32[32,1408]{1,0:T(8,128)} %embed_ref.1) | copy-start | bytes 540676
  11.9 29.1 %copy-start.8 = (f32[1,512]{1,0:T(1,128)S(1)}, f32[1,512]{1,0:T(1,128)}, u32[]{:S(2)}) copy-start(f32[1,512]{1,0:T(1,128)} %text_ref.1) | copy-start | bytes 6148
  11.9 29.1 %copy-start.9 = (s32[1,32]{1,0:T(1,128)S(1)}, s32[1,32]{1,0:T(1,128)}, u32[]{:S(2)}) copy-start(s32[1,32]{1,0:T(1,128)} %times_ref.3) | copy-start | bytes 388

commit v3 on v2

--- a/solution.py
+++ b/solution.py
@@ -107,11 +107,15 @@
     )
 
 
-def spatial_norm(count_ref, tok_ref, xn_ref, inverse_ref, info_ref):
+def clip_info(patches, count_ref, info_ref):
     count = count_ref[...].astype(f32)
     info_ref[0:1, :] = jnp.broadcast_to(count, (1, info_ref.shape[1]))
-    scale = 1.0 / (count * float(tok_ref.shape[1]))
+    scale = 1.0 / (count * float(patches))
     info_ref[1:2, :] = jnp.broadcast_to(scale, (1, info_ref.shape[1]))
+
+
+def spatial_norm(info_ref, tok_ref, xn_ref, inverse_ref):
+    del info_ref
     for frame in range(tok_ref.shape[0]):
         normed, inverse = normalize(tok_ref[frame].astype(f32))
         xn_ref[frame] = normed.astype(bf16)
@@ -480,19 +484,27 @@
     params = pltpu.CompilerParams(vmem_limit_bytes=20 * MIB)
     spatial_qkv = spatial_qkv.T
     temporal_qkv = temporal_qkv.T
-    xn, xn_inverse, info = pl.pallas_call(
+    info = pl.pallas_call(
+        functools.partial(clip_info, patches),
+        out_shape=shape((GROUP, LANES), f32),
+        in_specs=[VMEM],
+        out_specs=VMEM,
+        compiler_params=params,
+        cost_estimate=cost(30),
+        name="clip_info",
+    )(valid_count.reshape(1, 1))
+    xn, xn_inverse = pl.pallas_call(
         spatial_norm,
         out_shape=(
             shape(frames_in.shape, bf16),
             shape((local_frames, patches, 1), f32),
-            shape((GROUP, LANES), f32),
         ),
         in_specs=[VMEM] * 2,
-        out_specs=(VMEM,) * 3,
+        out_specs=(VMEM,) * 2,
         compiler_params=params,
-        cost_estimate=cost(30),
+        cost_estimate=cost(2),
         name="spatial_norm",
-    )(valid_count.reshape(1, 1), frames_in)
+    )(info, frames_in)
     part = shape((local_frames, patches, INNER), bf16)
     q, k, v, p, so = pl.pallas_call(
         spatial_attention,
@@ -506,7 +518,7 @@
         in_specs=[VMEM] * 2,
         out_specs=(VMEM,) * 5,
         compiler_params=params,
-        cost_estimate=cost(8),
+        cost_estimate=cost(30),
         name="spatial_attention",
     )(xn, spatial_qkv)
     x1 = pl.pallas_call(

time: 109 us -> 108 us (level)
  no operation moved by 1% of the time
where the time goes in v3:
time: 108 us
  blocking collectives  71.6 us (66%)
  Pallas kernels  32 us (30%)
  local copies, waits for them, and re-layouts  2.23 us (2%)
  between operations  1.62 us (2%)
    all_to_all x1, blocking collectives, per_device(): x1 = lax.all_to_all(x1, 'frame', split_axis=0, concat_axis=0, tiled=True)  29 us
    all_to_all x1, blocking collectives, per_device(): lax.all_to_all(grad_x1.reshape(traded), 'frame', split_axis=0, concat_axi...  24.4 us
    all_to_all x1, blocking collectives, per_device(): lax.all_to_all(send, ('frame', 'batch'), split_axis=0, concat_axis=0, til...  18.3 us
    pallas_call x1, Pallas kernels, per_device(): pl.pallas_call(spatial_backward, out_shape=(shape(frames_in.shape, bf16),...  9.76 us
    pallas_call x1, Pallas kernels, per_device(): pl.pallas_call(functools.partial(temporal_backward, clips, float(slots *...  7.92 us
    pallas_call x1, Pallas kernels, per_device(): pl.pallas_call(temporal_forward, out_shape=(shape((devices, 1, embed_size...  6.85 us
    pallas_call x1, Pallas kernels, per_device(): pl.pallas_call(spatial_attention, out_shape=(part, part, part, shape((loc...  5.15 us
    unnamed x20, local copies, waits for them, and re-layouts  2.23 us

profile of v3, /device:TPU:0, one launch (start us, length us, event | category | flops | bytes accessed | tf_op | source)
XLA Modules:
  0.0 107.5 jit_solution(9493189878482330633)
XLA Ops:
  1.3 0.0 copy-start.3
  1.3 0.0 copy-start
  1.3 0.1 clip_info.1.info_ref
  1.4 1.3 %copy-done.3 = bf16[1,2,256,1408]{3,2,1,0:T(8,128)(2,1)S(1)} copy-done((bf16[1,2,256,1408]{3,2,1,0:T(8,128)(2,1)S(1)}, bf16[1,2,256,1408]{3,2,1,0:T(8,128)(2,1)}, u32[]{:S(2)}) %copy-start.3) | copy-done | bytes 1441816
  2.6 0.0 slice-start
  2.6 0.9 spatial_norm.1
  3.5 0.9 copy-done
  4.4 0.0 copy-start.2
  4.4 0.0 slice-start.1
  4.4 5.2 %spatial_attention.1 = (bf16[2,256,704]{2,1,0:T(8,128)(2,1)S(1)}, bf16[2,256,704]{2,1,0:T(8,128)(2,1)S(1)}, bf16[2,256,704]{2,1,0:T(8,128)(2,1)S(1)}, bf16[2,8,2...) custom-call(bf16[2,256,1408]{2,1,0:T(8,128)(2,1)S(1)} %get-tuple-element.20.xn_ref, bf16[2112,1408]{1,0:T(8,128)(2,1)S(1)} %bitcast.15), custom_call_target="tpu_custom_call" | custom-call | flops 30000001024 | tf_op jit(solution)/shard_map/spatial_attention/pallas_call | solution.py:509
  9.6 0.0 copy-done.2
  9.6 0.0 copy-start.4
  9.6 1.4 %spatial_output.1 = bf16[16,32,1408]{2,1,0:T(8,128)(2,1)S(1)} custom-call(bf16[2,256,1408]{2,1,0:T(8,128)(2,1)S(1)} %bitcast.18, bf16[2,256,704]{2,1,0:T(8,128)(2,1)S(1)} %get-tuple-element.21.so_ref, bf16[704,1408]{1,0:T(8,128)(2,1)S(1)} %copy-done.2), custom_call_target="tpu_custom_call" | custom-call | flops 2000000000 | tf_op jit(solution)/shard_map/spatial_output/pallas_call | solution.py:524
  11.0 0.0 copy-start.1
  11.0 0.0 copy-start.5
  11.0 0.0 copy-start.6
  11.1 0.0 copy-start.7
  11.1 29.0 %all_to_all.15 = bf16[16,32,1408]{2,1,0:T(8,128)(2,1)S(1)} all-to-all(bf16[16,32,1408]{2,1,0:T(8,128)(2,1)S(1)} %spatial_output.1), channel_id=1, replica_groups=mesh['batch'=8,'frame'=16] {'frame'}, dimensions={0} | all-to-all | bytes 2883584 | tf_op jit(solution)/shard_map/all_to_all | solution.py:534
  40.0 0.0 slice-done
  40.0 0.0 slice-done.1
  40.0 0.0 copy-done.4
  40.0 0.0 copy-done.1
  40.0 0.0 copy-done.5
  40.1 0.0 copy-done.6
  40.1 0.0 copy-done.7
  40.1 6.9 %temporal_forward.1 = (f32[128,1,640]{2,1,0:T(1,128)S(1)}, bf16[512,1408]{1,0:T(8,128)(2,1)S(1)}, f32[512,1]{1,0:T(8,128)S(1)}, bf16[512,704]{1,0:T(8,128)(2,1)S...) custom-call(f32[8,128]{1,0:T(8,128)S(1)} %clip_info.1.info_ref, ...), custom_call_target="tpu_custom_call" | custom-call | flops 7000000000 | tf_op jit(solution)/shard_map/temporal_forward/pallas_call | solution.py:537
  46.9 18.3 %all_to_all.16.parts_ref = f32[128,1,640]{2,1,0:T(1,128)S(1)} all-to-all(f32[128,1,640]{2,1,0:T(1,128)S(1)} %get-tuple-element.22), channel_id=1, replica_groups=mesh['batch'=8,'frame'=16] {'frame','batch'}, dimensions={0} | all-to-all | bytes 655360 | tf_op jit(solution)/shard_map/all_to_all | solution.py:564
  65.2 7.9 %temporal_backward.1 = (bf16[32,16,1408]{2,1,0:T(8,128)(2,1)S(1)}, f32[8,128]{1,0:T(8,128)S(1)}) custom-call(f32[8,128]{1,0:T(8,128)S(1)} %clip_info.1.info_ref, s32[1,32]{1,0:T(1,128)S(1)} %copy-done.7, f32[128,1,640]{2,1,0:T(1,128)S(1)} %all_to_all.16.parts_ref, bf16[512,1408]{1,0:T(8,128)(2,1)S(1)} %get-tuple-element.23.tn_ref, ...), custom_call_target="tpu_custom_call" | custom-call | flops 8000000000 | tf_op jit(solution)/shard_map/temporal_backward/pallas_call | solution.py:565
  73.2 24.4 %all_to_all.17.grad_ref = bf16[16,32,1408]{2,1,0:T(8,128)(2,1)S(1)} all-to-all(bf16[16,32,1408]{2,1,0:T(8,128)(2,1)S(1)} %bitcast.9), channel_id=1, replica_groups=mesh['batch'=8,'frame'=16] {'frame'}, dimensions={0} | all-to-all | bytes 2883584 | tf_op jit(solution)/shard_map/all_to_all | solution.py:588
  97.6 9.8 %spatial_backward.1 = (bf16[2,256,1408]{2,1,0:T(8,128)(2,1)}, f32[1,1]{1,0:T(1,128)}) custom-call(bf16[16,32,1408]{2,1,0:T(8,128)(2,1)S(1)} %all_to_all.17.grad_ref, bf16[2,256,1408]{2,1,0:T(8,128)(2,1)S(1)} %get-tuple-element.20.xn_ref, f32[2,256,1]{2,1,0:T(8,128)S(1)} %get-tuple-element.30.inverse_ref, bf16[2112,1408]{1,0:T(8,128)(2,1)S(1)} %bitcast.16, ...), custom_call_target="tpu_custom_call" | custom-call | flops 12000000000 | tf_op jit(solution)/shard_map/spatial_backward/pallas_call | solution.py:591
  (1 shorter events, 0.0 us)
Async XLA Ops:
  1.3 1.4 %copy-start.3 = (bf16[1,2,256,1408]{3,2,1,0:T(8,128)(2,1)S(1)}, bf16[1,2,256,1408]{3,2,1,0:T(8,128)(2,1)}, u32[]{:S(2)}) copy-start(bf16[1,2,256,1408]{3,2,1,0:T(8,128)(2,1)} %param.10) | copy-start | bytes 4325380
  1.3 3.1 %copy-start = (bf16[1408,2112]{0,1:T(8,128)(2,1)S(1)}, bf16[1408,2112]{0,1:T(8,128)(2,1)}, u32[]{:S(2)}) copy-start(bf16[1408,2112]{0,1:T(8,128)(2,1)} %param.13) | copy-start | bytes 17842180
  2.6 37.4 %slice-start = ((s8[5947392]{0:T(1024)(128)(4,1)}), s8[4194304]{0:T(1024)(128)(4,1)S(1)}, s32[]{:S(2)}) async-start(s8[5947392]{0:T(1024)(128)(4,1)} %bitcast.11), calls=%async_computation.3 | async-start | bytes 8388608
  4.4 5.2 %copy-start.2 = (bf16[704,1408]{1,0:T(8,128)(2,1)S(1)}, bf16[704,1408]{1,0:T(8,128)(2,1)}, u32[]{:S(2)}) copy-start(bf16[704,1408]{1,0:T(8,128)(2,1)} %out_ref.7) | copy-start | bytes 5947396
  4.4 35.6 %slice-start.1 = ((s8[5947392]{0:T(1024)(128)(4,1)}), s8[1753088]{0:T(1024)(128)(4,1)S(1)}, s32[]{:S(2)}) async-start(s8[5947392]{0:T(1024)(128)(4,1)} %bitcast.11), calls=%async_computation.4 | async-start | bytes 3506176
  9.6 30.4 %copy-start.4 = (bf16[1408,512]{1,0:T(8,128)(2,1)S(1)}, bf16[1408,512]{1,0:T(8,128)(2,1)}, u32[]{:S(2)}) copy-start(bf16[1408,512]{1,0:T(8,128)(2,1)} %proj_ref.3) | copy-start | bytes 4325380
  11.0 29.0 %copy-start.1 = (bf16[704,1408]{1,0:T(8,128)(2,1)S(1)}, bf16[704,1408]{1,0:T(8,128)(2,1)}, u32[]{:S(2)}) copy-start(bf16[704,1408]{1,0:T(8,128)(2,1)} %out_ref.6) | copy-start | bytes 5947396
  11.0 29.0 %copy-start.5 = (f32[32,1408]{1,0:T(8,128)S(1)}, f32[32,1408]{1,0:T(8,128)}, u32[]{:S(2)}) copy-start(f32[32,1408]{1,0:T(8,128)} %embed_ref.1) | copy-start | bytes 540676
  11.0 29.0 %copy-start.6 = (f32[1,512]{1,0:T(1,128)S(1)}, f32[1,512]{1,0:T(1,128)}, u32[]{:S(2)}) copy-start(f32[1,512]{1,0:T(1,128)} %text_ref.1) | copy-start | bytes 6148
  11.1 29.0 %copy-start.7 = (s32[1,32]{1,0:T(1,128)S(1)}, s32[1,32]{1,0:T(1,128)}, u32[]{:S(2)}) copy-start(s32[1,32]{1,0:T(1,128)} %times_ref.3) | copy-start | bytes 388

commit v4 on v3

--- a/solution.py
+++ b/solution.py
@@ -13,6 +13,7 @@
 INNER = HEADS * HD
 LANES = 128
 GROUP = 8
+SPLIT = 512
 PIECES = 4
 EPSILON = 1e-06
 SHARPNESS = 1.0 / 0.07
@@ -372,16 +373,11 @@
     )
     e, inverse_z = unit_rows(z)
     u, _ = unit_rows(text)
-    logits = (
-        lax.dot_general(
-            e,
-            u,
-            (((1,), (1,)), ((), ())),
-            precision=lax.Precision.HIGHEST,
-            preferred_element_type=f32,
-        )
-        * SHARPNESS
-    )
+    column = lax.broadcasted_iota(jnp.int32, (clips, clips), 1)
+    logits = jnp.zeros((clips, clips), f32)
+    for j in range(clips):
+        product = jnp.sum(e * u[j : j + 1], axis=1, keepdims=True) * SHARPNESS
+        logits = jnp.where(column == j, product, logits)
     raised = jnp.exp(logits)
     row_total = jnp.sum(raised, axis=1, keepdims=True)
     column_total = jnp.sum(raised, axis=0, keepdims=True)
@@ -395,13 +391,10 @@
     )
     loss_ref[...] = jnp.broadcast_to(loss, loss_ref.shape)
     shares = 0.5 * (raised / row_total + raised / column_total) - jnp.where(diagonal, 1.0, 0.0)
-    grad_e = (cotangent * SHARPNESS) * lax.dot_general(
-        shares,
-        u,
-        (((1,), (0,)), ((), ())),
-        precision=lax.Precision.HIGHEST,
-        preferred_element_type=f32,
-    )
+    shares = shares * (cotangent * SHARPNESS)
+    grad_e = shares[:, 0:1] * u[0:1]
+    for j in range(1, clips):
+        grad_e = grad_e + shares[:, j : j + 1] * u[j : j + 1]
     grad_z = inverse_z * (grad_e - e * jnp.sum(e * grad_e, axis=-1, keepdims=True))
     own = lax.broadcasted_iota(jnp.int32, grad_z.shape, 0) == lax.axis_index("batch")
     grad_own = jnp.sum(jnp.where(own, grad_z, 0.0), axis=0, keepdims=True)
@@ -437,8 +430,11 @@
         weights_c = jnp.concatenate([c_high[:, own], c_high[:, own], c_low[:, own]], axis=0)
         value_rows = jnp.concatenate([high, low, high], axis=0)
         grad_tn = dot_nn((merge_heads(dq) * SCALE).astype(bf16), qkv_ref[:INNER, :])
-        grad_tn += dot_nn((merge_heads(dk) * KEY_BACK).astype(bf16), qkv_ref[INNER : 2 * INNER, :])
-        dtn_ref[at, :] = grad_tn + dot_tn(weights_c, value_rows)
+        dk = (merge_heads(dk) * KEY_BACK).astype(bf16)
+        grad_tn += dot_nn(dk[:, :SPLIT], qkv_ref[INNER : INNER + SPLIT, :])
+        last = jnp.concatenate([dk[:, SPLIT:], weights_c.astype(f32).T.astype(bf16)], axis=1)
+        rest_rows = jnp.concatenate([qkv_ref[INNER + SPLIT : 2 * INNER, :], value_rows], axis=0)
+        dtn_ref[at, :] = grad_tn + dot_nn(last, rest_rows)
     chunk = 8
     for start in range(0, slots, chunk):
         pieces = []

time: 108 us -> 107 us (level)
  no operation moved by 1% of the time
where the time goes in v4:
time: 107 us
  blocking collectives  71.7 us (67%)
  Pallas kernels  31.5 us (29%)
  local copies, waits for them, and re-layouts  2.23 us (2%)
  between operations  1.6 us (1%)
    all_to_all x1, blocking collectives, per_device(): x1 = lax.all_to_all(x1, 'frame', split_axis=0, concat_axis=0, tiled=True)  29 us
    all_to_all x1, blocking collectives, per_device(): lax.all_to_all(grad_x1.reshape(traded), 'frame', split_axis=0, concat_axi...  24.4 us
    all_to_all x1, blocking collectives, per_device(): lax.all_to_all(send, ('frame', 'batch'), split_axis=0, concat_axis=0, til...  18.3 us
    pallas_call x1, Pallas kernels, per_device(): pl.pallas_call(spatial_backward, out_shape=(shape(frames_in.shape, bf16),...  9.76 us
    pallas_call x1, Pallas kernels, per_device(): pl.pallas_call(functools.partial(temporal_backward, clips, float(slots *...  7.43 us
    pallas_call x1, Pallas kernels, per_device(): pl.pallas_call(temporal_forward, out_shape=(shape((devices, 1, embed_size...  6.85 us
    pallas_call x1, Pallas kernels, per_device(): pl.pallas_call(spatial_attention, out_shape=(part, part, part, shape((loc...  5.15 us
    unnamed x20, local copies, waits for them, and re-layouts  2.23 us

profile of v4, /device:TPU:0, one launch (start us, length us, event | category | flops | bytes accessed | tf_op | source)
XLA Modules:
  0.0 107.0 jit_solution(3119352547150710214)
XLA Ops:
  1.3 0.0 copy-start.3
  1.3 0.0 copy-start
  1.3 0.1 clip_info.1.info_ref
  1.4 1.3 %copy-done.3 = bf16[1,2,256,1408]{3,2,1,0:T(8,128)(2,1)S(1)} copy-done((bf16[1,2,256,1408]{3,2,1,0:T(8,128)(2,1)S(1)}, bf16[1,2,256,1408]{3,2,1,0:T(8,128)(2,1)}, u32[]{:S(2)}) %copy-start.3) | copy-done | bytes 1441816
  2.6 0.0 slice-start
  2.6 0.9 spatial_norm.1
  3.5 0.9 copy-done
  4.4 0.0 copy-start.2
  4.4 0.0 slice-start.1
  4.4 5.2 %spatial_attention.1 = (bf16[2,256,704]{2,1,0:T(8,128)(2,1)S(1)}, bf16[2,256,704]{2,1,0:T(8,128)(2,1)S(1)}, bf16[2,256,704]{2,1,0:T(8,128)(2,1)S(1)}, bf16[2,8,2...) custom-call(bf16[2,256,1408]{2,1,0:T(8,128)(2,1)S(1)} %get-tuple-element.20.xn_ref, bf16[2112,1408]{1,0:T(8,128)(2,1)S(1)} %bitcast.15), custom_call_target="tpu_custom_call" | custom-call | flops 30000001024 | tf_op jit(solution)/shard_map/spatial_attention/pallas_call | solution.py:505
  9.6 0.0 copy-done.2
  9.6 0.0 copy-start.4
  9.6 1.4 %spatial_output.1 = bf16[16,32,1408]{2,1,0:T(8,128)(2,1)S(1)} custom-call(bf16[2,256,1408]{2,1,0:T(8,128)(2,1)S(1)} %bitcast.18, bf16[2,256,704]{2,1,0:T(8,128)(2,1)S(1)} %get-tuple-element.21.so_ref, bf16[704,1408]{1,0:T(8,128)(2,1)S(1)} %copy-done.2), custom_call_target="tpu_custom_call" | custom-call | flops 2000000000 | tf_op jit(solution)/shard_map/spatial_output/pallas_call | solution.py:520
  11.0 0.0 copy-start.1
  11.0 0.0 copy-start.5
  11.0 0.0 copy-start.6
  11.1 0.0 copy-start.7
  11.1 29.0 %all_to_all.15 = bf16[16,32,1408]{2,1,0:T(8,128)(2,1)S(1)} all-to-all(bf16[16,32,1408]{2,1,0:T(8,128)(2,1)S(1)} %spatial_output.1), channel_id=1, replica_groups=mesh['batch'=8,'frame'=16] {'frame'}, dimensions={0} | all-to-all | bytes 2883584 | tf_op jit(solution)/shard_map/all_to_all | solution.py:530
  40.0 0.0 slice-done
  40.0 0.0 slice-done.1
  40.0 0.0 copy-done.4
  40.0 0.0 copy-done.1
  40.0 0.0 copy-done.5
  40.1 0.0 copy-done.6
  40.1 0.0 copy-done.7
  40.1 6.9 %temporal_forward.1 = (f32[128,1,640]{2,1,0:T(1,128)S(1)}, bf16[512,1408]{1,0:T(8,128)(2,1)S(1)}, f32[512,1]{1,0:T(8,128)S(1)}, bf16[512,704]{1,0:T(8,128)(2,1)S...) custom-call(f32[8,128]{1,0:T(8,128)S(1)} %clip_info.1.info_ref, ...), custom_call_target="tpu_custom_call" | custom-call | flops 7000000000 | tf_op jit(solution)/shard_map/temporal_forward/pallas_call | solution.py:533
  46.9 18.3 %all_to_all.16.parts_ref = f32[128,1,640]{2,1,0:T(1,128)S(1)} all-to-all(f32[128,1,640]{2,1,0:T(1,128)S(1)} %get-tuple-element.22), channel_id=1, replica_groups=mesh['batch'=8,'frame'=16] {'frame','batch'}, dimensions={0} | all-to-all | bytes 655360 | tf_op jit(solution)/shard_map/all_to_all | solution.py:560
  65.2 7.4 %temporal_backward.1 = (bf16[32,16,1408]{2,1,0:T(8,128)(2,1)S(1)}, f32[8,128]{1,0:T(8,128)S(1)}) custom-call(f32[8,128]{1,0:T(8,128)S(1)} %clip_info.1.info_ref, s32[1,32]{1,0:T(1,128)S(1)} %copy-done.7, f32[128,1,640]{2,1,0:T(1,128)S(1)} %all_to_all.16.parts_ref, bf16[512,1408]{1,0:T(8,128)(2,1)S(1)} %get-tuple-element.23.tn_ref, ...), custom_call_target="tpu_custom_call" | custom-call | flops 8000000000 | tf_op jit(solution)/shard_map/temporal_backward/pallas_call | solution.py:561
  72.7 24.4 %all_to_all.17.grad_ref = bf16[16,32,1408]{2,1,0:T(8,128)(2,1)S(1)} all-to-all(bf16[16,32,1408]{2,1,0:T(8,128)(2,1)S(1)} %bitcast.9), channel_id=1, replica_groups=mesh['batch'=8,'frame'=16] {'frame'}, dimensions={0} | all-to-all | bytes 2883584 | tf_op jit(solution)/shard_map/all_to_all | solution.py:584
  97.1 9.8 %spatial_backward.1 = (bf16[2,256,1408]{2,1,0:T(8,128)(2,1)}, f32[1,1]{1,0:T(1,128)}) custom-call(bf16[16,32,1408]{2,1,0:T(8,128)(2,1)S(1)} %all_to_all.17.grad_ref, bf16[2,256,1408]{2,1,0:T(8,128)(2,1)S(1)} %get-tuple-element.20.xn_ref, f32[2,256,1]{2,1,0:T(8,128)S(1)} %get-tuple-element.30.inverse_ref, bf16[2112,1408]{1,0:T(8,128)(2,1)S(1)} %bitcast.16, ...), custom_call_target="tpu_custom_call" | custom-call | flops 12000000000 | tf_op jit(solution)/shard_map/spatial_backward/pallas_call | solution.py:587
  (1 shorter events, 0.0 us)
Async XLA Ops:
  1.3 1.4 %copy-start.3 = (bf16[1,2,256,1408]{3,2,1,0:T(8,128)(2,1)S(1)}, bf16[1,2,256,1408]{3,2,1,0:T(8,128)(2,1)}, u32[]{:S(2)}) copy-start(bf16[1,2,256,1408]{3,2,1,0:T(8,128)(2,1)} %param.10) | copy-start | bytes 4325380
  1.3 3.1 %copy-start = (bf16[1408,2112]{0,1:T(8,128)(2,1)S(1)}, bf16[1408,2112]{0,1:T(8,128)(2,1)}, u32[]{:S(2)}) copy-start(bf16[1408,2112]{0,1:T(8,128)(2,1)} %param.13) | copy-start | bytes 17842180
  2.6 37.4 %slice-start = ((s8[5947392]{0:T(1024)(128)(4,1)}), s8[4194304]{0:T(1024)(128)(4,1)S(1)}, s32[]{:S(2)}) async-start(s8[5947392]{0:T(1024)(128)(4,1)} %bitcast.11), calls=%async_computation.3 | async-start | bytes 8388608
  4.4 5.2 %copy-start.2 = (bf16[704,1408]{1,0:T(8,128)(2,1)S(1)}, bf16[704,1408]{1,0:T(8,128)(2,1)}, u32[]{:S(2)}) copy-start(bf16[704,1408]{1,0:T(8,128)(2,1)} %out_ref.7) | copy-start | bytes 5947396
  4.4 35.6 %slice-start.1 = ((s8[5947392]{0:T(1024)(128)(4,1)}), s8[1753088]{0:T(1024)(128)(4,1)S(1)}, s32[]{:S(2)}) async-start(s8[5947392]{0:T(1024)(128)(4,1)} %bitcast.11), calls=%async_computation.4 | async-start | bytes 3506176
  9.6 30.4 %copy-start.4 = (bf16[1408,512]{1,0:T(8,128)(2,1)S(1)}, bf16[1408,512]{1,0:T(8,128)(2,1)}, u32[]{:S(2)}) copy-start(bf16[1408,512]{1,0:T(8,128)(2,1)} %proj_ref.3) | copy-start | bytes 4325380
  11.0 29.0 %copy-start.1 = (bf16[704,1408]{1,0:T(8,128)(2,1)S(1)}, bf16[704,1408]{1,0:T(8,128)(2,1)}, u32[]{:S(2)}) copy-start(bf16[704,1408]{1,0:T(8,128)(2,1)} %out_ref.6) | copy-start | bytes 5947396
  11.0 29.0 %copy-start.5 = (f32[32,1408]{1,0:T(8,128)S(1)}, f32[32,1408]{1,0:T(8,128)}, u32[]{:S(2)}) copy-start(f32[32,1408]{1,0:T(8,128)} %embed_ref.1) | copy-start | bytes 540676
  11.0 29.0 %copy-start.6 = (f32[1,512]{1,0:T(1,128)S(1)}, f32[1,512]{1,0:T(1,128)}, u32[]{:S(2)}) copy-start(f32[1,512]{1,0:T(1,128)} %text_ref.1) | copy-start | bytes 6148
  11.1 29.0 %copy-start.7 = (s32[1,32]{1,0:T(1,128)S(1)}, s32[1,32]{1,0:T(1,128)}, u32[]{:S(2)}) copy-start(s32[1,32]{1,0:T(1,128)} %times_ref.3) | copy-start | bytes 388

commit v5 on v4

--- a/solution.py
+++ b/solution.py
@@ -182,32 +182,41 @@
     owners = grad_ref.shape[0]
     share = patches // owners
     copies = []
-    for frame in range(frames):
-        own = slice(frame * share, (frame + 1) * share)
-        grad_x1 = grad_ref[:, own, :].reshape(patches, width)
+
+    def rows_of(frame):
+        return slice(frame * share, (frame + 1) * share)
+
+    def first_products(frame):
+        grad_x1 = grad_ref[:, rows_of(frame), :].reshape(patches, width)
         grad_so = dot_nt(grad_x1, out_ref[...]).astype(bf16)
-        dv = []
+        dv, grad_weights, inner = [], [], []
         for head in range(HEADS):
             first, last, _ = window(head)
             dv.append(dot_tn(p_ref[frame, head], grad_so[:, first:last]))
-        dv = merge_heads(dv).astype(bf16)
-        grad_weights, inner = [], []
         for head in range(HEADS):
             first, last, _ = window(head)
             grad_head = keep_head(grad_so[:, first:last], head)
             along = grad_head.astype(f32) * so_ref[frame, :, first:last].astype(f32)
             inner.append(jnp.sum(along, axis=-1, keepdims=True))
             grad_weights.append(dot_nt(grad_head, v_ref[frame, :, first:last]))
+        return merge_heads(dv).astype(bf16), grad_weights, inner
+
+    def score_grads(frame, grad_weights, inner):
+        grad_scores = []
+        for head in range(HEADS):
+            weights = p_ref[frame, head].astype(f32)
+            grad_scores.append((weights * (grad_weights[head] - inner[head])).astype(bf16))
+        return grad_scores
+
+    def second_products(frame, grad_scores):
         dq, dk = [], []
         for head in range(HEADS):
             first, last, _ = window(head)
-            weights = p_ref[frame, head].astype(f32)
-            grad_scores = (weights * (grad_weights[head] - inner[head])).astype(bf16)
-            dq.append(dot_nn(grad_scores, k_ref[frame, :, first:last]))
-            dk.append(dot_tn(grad_scores, q_ref[frame, :, first:last]))
-        grad_xn = dot_nn((merge_heads(dq) * SCALE).astype(bf16), qkv_ref[:INNER, :])
-        grad_xn += dot_nn((merge_heads(dk) * KEY_BACK).astype(bf16), qkv_ref[INNER : 2 * INNER, :])
-        grad_xn += dot_nn(dv, qkv_ref[2 * INNER :, :])
+            dq.append(dot_nn(grad_scores[head], k_ref[frame, :, first:last]))
+            dk.append(dot_tn(grad_scores[head], q_ref[frame, :, first:last]))
+        return (merge_heads(dq) * SCALE).astype(bf16), (merge_heads(dk) * KEY_BACK).astype(bf16)
+
+    def finish(frame, grad_xn):
         for piece in range(PIECES):
             size = patches // PIECES
             at = slice(piece * size, (piece + 1) * size)
@@ -215,7 +224,7 @@
                 grad_xn[at], xn_ref[frame, at].astype(f32), inverse_ref[frame, at]
             )
             held = slice(piece * owners // PIECES, (piece + 1) * owners // PIECES)
-            grad_x1 = grad_ref[held, own, :].reshape(size, width)
+            grad_x1 = grad_ref[held, rows_of(frame), :].reshape(size, width)
             result_ref[frame, at] = (grad_x1.astype(f32) + back).astype(bf16)
             rows = pl.ds(piece * size, size)
             copy = pltpu.make_async_copy(
@@ -225,6 +234,21 @@
             )
             copy.start()
             copies.append(copy)
+
+    waiting = first_products(0)
+    before = None
+    for frame in range(frames):
+        dv, grad_weights, inner = waiting
+        grad_scores = score_grads(frame, grad_weights, inner)
+        if frame + 1 < frames:
+            waiting = first_products(frame + 1)
+        dq, dk = second_products(frame, grad_scores)
+        if before is not None:
+            finish(frame - 1, before)
+        before = dot_nn(dq, qkv_ref[:INNER, :])
+        before += dot_nn(dk, qkv_ref[INNER : 2 * INNER, :])
+        before += dot_nn(dv, qkv_ref[2 * INNER :, :])
+    finish(frames - 1, before)
     for copy in copies + [loss_copy]:
         copy.wait()
 

time: 107 us -> 107 us (level)
  no operation moved by 1% of the time
where the time goes in v5:
time: 107 us
  blocking collectives  71.7 us (67%)
  Pallas kernels  31.4 us (29%)
  local copies, waits for them, and re-layouts  2.23 us (2%)
  between operations  1.6 us (1%)
    all_to_all x1, blocking collectives, per_device(): x1 = lax.all_to_all(x1, 'frame', split_axis=0, concat_axis=0, tiled=True)  29 us
    all_to_all x1, blocking collectives, per_device(): lax.all_to_all(grad_x1.reshape(traded), 'frame', split_axis=0, concat_axi...  24.4 us
    all_to_all x1, blocking collectives, per_device(): lax.all_to_all(send, ('frame', 'batch'), split_axis=0, concat_axis=0, til...  18.3 us
    pallas_call x1, Pallas kernels, per_device(): pl.pallas_call(spatial_backward, out_shape=(shape(frames_in.shape, bf16),...  9.64 us
    pallas_call x1, Pallas kernels, per_device(): pl.pallas_call(functools.partial(temporal_backward, clips, float(slots *...  7.43 us
    pallas_call x1, Pallas kernels, per_device(): pl.pallas_call(temporal_forward, out_shape=(shape((devices, 1, embed_size...  6.85 us
    pallas_call x1, Pallas kernels, per_device(): pl.pallas_call(spatial_attention, out_shape=(part, part, part, shape((loc...  5.15 us
    unnamed x20, local copies, waits for them, and re-layouts  2.23 us

profile of v5, /device:TPU:0, one launch (start us, length us, event | category | flops | bytes accessed | tf_op | source)
XLA Modules:
  0.0 106.9 jit_solution(18228035279688931161)
XLA Ops:
  1.3 0.0 copy-start.3
  1.3 0.0 copy-start
  1.3 0.1 clip_info.1.info_ref
  1.4 1.3 %copy-done.3 = bf16[1,2,256,1408]{3,2,1,0:T(8,128)(2,1)S(1)} copy-done((bf16[1,2,256,1408]{3,2,1,0:T(8,128)(2,1)S(1)}, bf16[1,2,256,1408]{3,2,1,0:T(8,128)(2,1)}, u32[]{:S(2)}) %copy-start.3) | copy-done | bytes 1441816
  2.6 0.0 slice-start
  2.6 0.9 spatial_norm.1
  3.5 0.9 copy-done
  4.4 0.0 copy-start.2
  4.4 0.0 slice-start.1
  4.4 5.2 %spatial_attention.1 = (bf16[2,256,704]{2,1,0:T(8,128)(2,1)S(1)}, bf16[2,256,704]{2,1,0:T(8,128)(2,1)S(1)}, bf16[2,256,704]{2,1,0:T(8,128)(2,1)S(1)}, bf16[2,8,2...) custom-call(bf16[2,256,1408]{2,1,0:T(8,128)(2,1)S(1)} %get-tuple-element.20.xn_ref, bf16[2112,1408]{1,0:T(8,128)(2,1)S(1)} %bitcast.15), custom_call_target="tpu_custom_call" | custom-call | flops 30000001024 | tf_op jit(solution)/shard_map/spatial_attention/pallas_call | solution.py:529
  9.6 0.0 copy-done.2
  9.6 0.0 copy-start.4
  9.6 1.4 %spatial_output.1 = bf16[16,32,1408]{2,1,0:T(8,128)(2,1)S(1)} custom-call(bf16[2,256,1408]{2,1,0:T(8,128)(2,1)S(1)} %bitcast.18, bf16[2,256,704]{2,1,0:T(8,128)(2,1)S(1)} %get-tuple-element.21.so_ref, bf16[704,1408]{1,0:T(8,128)(2,1)S(1)} %copy-done.2), custom_call_target="tpu_custom_call" | custom-call | flops 2000000000 | tf_op jit(solution)/shard_map/spatial_output/pallas_call | solution.py:544
  11.0 0.0 copy-start.1
  11.0 0.0 copy-start.5
  11.0 0.0 copy-start.6
  11.1 0.0 copy-start.7
  11.1 29.0 %all_to_all.15 = bf16[16,32,1408]{2,1,0:T(8,128)(2,1)S(1)} all-to-all(bf16[16,32,1408]{2,1,0:T(8,128)(2,1)S(1)} %spatial_output.1), channel_id=1, replica_groups=mesh['batch'=8,'frame'=16] {'frame'}, dimensions={0} | all-to-all | bytes 2883584 | tf_op jit(solution)/shard_map/all_to_all | solution.py:554
  40.0 0.0 slice-done
  40.0 0.0 slice-done.1
  40.0 0.0 copy-done.4
  40.0 0.0 copy-done.1
  40.0 0.0 copy-done.5
  40.1 0.0 copy-done.6
  40.1 0.0 copy-done.7
  40.1 6.9 %temporal_forward.1 = (f32[128,1,640]{2,1,0:T(1,128)S(1)}, bf16[512,1408]{1,0:T(8,128)(2,1)S(1)}, f32[512,1]{1,0:T(8,128)S(1)}, bf16[512,704]{1,0:T(8,128)(2,1)S...) custom-call(f32[8,128]{1,0:T(8,128)S(1)} %clip_info.1.info_ref, ...), custom_call_target="tpu_custom_call" | custom-call | flops 7000000000 | tf_op jit(solution)/shard_map/temporal_forward/pallas_call | solution.py:557
  46.9 18.3 %all_to_all.16.parts_ref = f32[128,1,640]{2,1,0:T(1,128)S(1)} all-to-all(f32[128,1,640]{2,1,0:T(1,128)S(1)} %get-tuple-element.22), channel_id=1, replica_groups=mesh['batch'=8,'frame'=16] {'frame','batch'}, dimensions={0} | all-to-all | bytes 655360 | tf_op jit(solution)/shard_map/all_to_all | solution.py:584
  65.2 7.4 %temporal_backward.1 = (bf16[32,16,1408]{2,1,0:T(8,128)(2,1)S(1)}, f32[8,128]{1,0:T(8,128)S(1)}) custom-call(f32[8,128]{1,0:T(8,128)S(1)} %clip_info.1.info_ref, s32[1,32]{1,0:T(1,128)S(1)} %copy-done.7, f32[128,1,640]{2,1,0:T(1,128)S(1)} %all_to_all.16.parts_ref, bf16[512,1408]{1,0:T(8,128)(2,1)S(1)} %get-tuple-element.23.tn_ref, ...), custom_call_target="tpu_custom_call" | custom-call | flops 8000000000 | tf_op jit(solution)/shard_map/temporal_backward/pallas_call | solution.py:585
  72.7 24.4 %all_to_all.17.grad_ref = bf16[16,32,1408]{2,1,0:T(8,128)(2,1)S(1)} all-to-all(bf16[16,32,1408]{2,1,0:T(8,128)(2,1)S(1)} %bitcast.9), channel_id=1, replica_groups=mesh['batch'=8,'frame'=16] {'frame'}, dimensions={0} | all-to-all | bytes 2883584 | tf_op jit(solution)/shard_map/all_to_all | solution.py:608
  97.1 9.6 %spatial_backward.1 = (bf16[2,256,1408]{2,1,0:T(8,128)(2,1)}, f32[1,1]{1,0:T(1,128)}) custom-call(bf16[16,32,1408]{2,1,0:T(8,128)(2,1)S(1)} %all_to_all.17.grad_ref, bf16[2,256,1408]{2,1,0:T(8,128)(2,1)S(1)} %get-tuple-element.20.xn_ref, f32[2,256,1]{2,1,0:T(8,128)S(1)} %get-tuple-element.30.inverse_ref, bf16[2112,1408]{1,0:T(8,128)(2,1)S(1)} %bitcast.16, ...), custom_call_target="tpu_custom_call" | custom-call | flops 12000000000 | tf_op jit(solution)/shard_map/spatial_backward/pallas_call | solution.py:611
  (1 shorter events, 0.0 us)
Async XLA Ops:
  1.3 1.4 %copy-start.3 = (bf16[1,2,256,1408]{3,2,1,0:T(8,128)(2,1)S(1)}, bf16[1,2,256,1408]{3,2,1,0:T(8,128)(2,1)}, u32[]{:S(2)}) copy-start(bf16[1,2,256,1408]{3,2,1,0:T(8,128)(2,1)} %param.10) | copy-start | bytes 4325380
  1.3 3.1 %copy-start = (bf16[1408,2112]{0,1:T(8,128)(2,1)S(1)}, bf16[1408,2112]{0,1:T(8,128)(2,1)}, u32[]{:S(2)}) copy-start(bf16[1408,2112]{0,1:T(8,128)(2,1)} %param.13) | copy-start | bytes 17842180
  2.6 37.4 %slice-start = ((s8[5947392]{0:T(1024)(128)(4,1)}), s8[4194304]{0:T(1024)(128)(4,1)S(1)}, s32[]{:S(2)}) async-start(s8[5947392]{0:T(1024)(128)(4,1)} %bitcast.11), calls=%async_computation.3 | async-start | bytes 8388608
  4.4 5.2 %copy-start.2 = (bf16[704,1408]{1,0:T(8,128)(2,1)S(1)}, bf16[704,1408]{1,0:T(8,128)(2,1)}, u32[]{:S(2)}) copy-start(bf16[704,1408]{1,0:T(8,128)(2,1)} %out_ref.7) | copy-start | bytes 5947396
  4.4 35.6 %slice-start.1 = ((s8[5947392]{0:T(1024)(128)(4,1)}), s8[1753088]{0:T(1024)(128)(4,1)S(1)}, s32[]{:S(2)}) async-start(s8[5947392]{0:T(1024)(128)(4,1)} %bitcast.11), calls=%async_computation.4 | async-start | bytes 3506176
  9.6 30.4 %copy-start.4 = (bf16[1408,512]{1,0:T(8,128)(2,1)S(1)}, bf16[1408,512]{1,0:T(8,128)(2,1)}, u32[]{:S(2)}) copy-start(bf16[1408,512]{1,0:T(8,128)(2,1)} %proj_ref.3) | copy-start | bytes 4325380
  11.0 29.0 %copy-start.1 = (bf16[704,1408]{1,0:T(8,128)(2,1)S(1)}, bf16[704,1408]{1,0:T(8,128)(2,1)}, u32[]{:S(2)}) copy-start(bf16[704,1408]{1,0:T(8,128)(2,1)} %out_ref.6) | copy-start | bytes 5947396
  11.0 29.0 %copy-start.5 = (f32[32,1408]{1,0:T(8,128)S(1)}, f32[32,1408]{1,0:T(8,128)}, u32[]{:S(2)}) copy-start(f32[32,1408]{1,0:T(8,128)} %embed_ref.1) | copy-start | bytes 540676
  11.0 29.0 %copy-start.6 = (f32[1,512]{1,0:T(1,128)S(1)}, f32[1,512]{1,0:T(1,128)}, u32[]{:S(2)}) copy-start(f32[1,512]{1,0:T(1,128)} %text_ref.1) | copy-start | bytes 6148
  11.1 29.0 %copy-start.7 = (s32[1,32]{1,0:T(1,128)S(1)}, s32[1,32]{1,0:T(1,128)}, u32[]{:S(2)}) copy-start(s32[1,32]{1,0:T(1,128)} %times_ref.3) | copy-start | bytes 388
